TPU v7x, 32 devices: a whole 2x2x4 slice. The times are simulated.
32 devices in a mesh: stream: 2 (over x), batch: 16 (over z, y, core).
Axes of the slice: x: 2, y: 2, z: 4, core: 2. Of those that a mesh axis runs over, the one named last changes fastest.
Arguments:
- query_tokens: bfloat16 [4096, 768], P(('stream', 'batch')), may hold values from -6 to 6
- passage_tokens: bfloat16 [32768, 768], P(('stream', 'batch')), may hold values from -6 to 6
- query_lengths: int32 [64], P(('stream', 'batch')), may hold values from 8 to 64
- passage_lengths: int32 [64], P(('stream', 'batch')), may hold values from 64 to 512
- positives: int32 [64], replicated, may hold values from 0 to 63, each once
- w_query: bfloat16 [768, 768], replicated, may hold values from -0.21875 to 0.21875
- b_query: float32 [768], replicated, may hold values from -1.75 to 1.75
- w_key: bfloat16 [768, 768], replicated, may hold values from -0.21875 to 0.21875
- w_value: bfloat16 [768, 768], replicated, may hold values from -0.21875 to 0.21875
- b_value: float32 [768], replicated, may hold values from -0.0625 to 0.0625
- w_out: bfloat16 [768, 768], replicated, may hold values from -1.25 to 1.25
- b_out: float32 [768], replicated, may hold values from -0.1875 to 0.1875
- norm1_gain: float32 [768], replicated, may hold values from 0.5 to 1.5
- norm1_bias: float32 [768], replicated, may hold values from -0.1875 to 0.1875
- w_in: bfloat16 [768, 3072], replicated, may hold values from -0.21875 to 0.21875
- b_in: float32 [3072], replicated, may hold values from -0.625 to 0.625
- w_down: bfloat16 [3072, 768], replicated, may hold values from -0.109375 to 0.109375
- b_down: float32 [768], replicated, may hold values from -0.1875 to 0.1875
- norm2_gain: float32 [768], replicated, may hold values from 0.5 to 1.5
- norm2_bias: float32 [768], replicated, may hold values from -0.1875 to 0.1875
- query_out_grad: bfloat16 [4096, 768], P(('stream', 'batch')), may hold values from -6 to 6
- passage_out_grad: bfloat16 [32768, 768], P(('stream', 'batch')), may hold values from -6 to 6
Outputs:
- query_out: bfloat16 [4096, 768], P(('stream', 'batch'))
- passage_out: bfloat16 [32768, 768], P(('stream', 'batch'))
- query_input_grad: float32 [4096, 768], P(('stream', 'batch'))
- passage_input_grad: float32 [32768, 768], P(('stream', 'batch'))
- loss: float32 [], replicated
- grad_w_query: float32 [768, 768], replicated
- grad_b_query: float32 [768], replicated
- grad_w_key: float32 [768, 768], replicated
- grad_w_value: float32 [768, 768], replicated
- grad_b_value: float32 [768], replicated
- grad_w_out: float32 [768, 768], replicated
- grad_b_out: float32 [768], replicated
- grad_norm1_gain: float32 [768], replicated
- grad_norm1_bias: float32 [768], replicated
- grad_w_in: float32 [768, 3072], replicated
- grad_b_in: float32 [3072], replicated
- grad_w_down: float32 [3072, 768], replicated
- grad_b_down: float32 [768], replicated
- grad_norm2_gain: float32 [768], replicated
- grad_norm2_bias: float32 [768], replicated
Inputs may be any that keep to these rules, and one draw needn't show every extreme that they name: positives names every passage exactly once.
All inputs are finite; a program needn't handle non-finite values.
Results may differ from a plain program's by a relative error of at most 0.014.
Values may be sent and summed in bfloat16 or wider, within the bound.
No kernel may reach another device: no remote copies, remote signals or barrier semaphores. Data moves between devices by JAX's collectives and lax.ppermute only.
A program may use at most 192 MiB of HBM per device.

v0:
```python
import jax
import jax.numpy as jnp
from jax import lax
from jax.sharding import PartitionSpec as P

HEADS = 12
QRY_LEN = 64
PASS_LEN = 512


sharpness_divisor = 0.01
epsilon = 1e-06


def layer_norm(value, gain, offset):
    centred = value - jnp.mean(value, axis=-1, keepdims=True)
    variance = jnp.mean(centred * centred, axis=-1, keepdims=True)
    return centred * lax.rsqrt(variance + epsilon) * gain + offset


def unit_rows(value):
    return value * lax.rsqrt(jnp.sum(value * value, axis=-1, keepdims=True) + epsilon)


def gelu_exact(value):
    return jax.nn.gelu(value, approximate=False)


def right_mul(left, weight):
    return jnp.dot(left, weight, preferred_element_type=jnp.float32)


def weight_grad(left, right):
    return jnp.einsum("ta,tb->ab", left, right, preferred_element_type=jnp.float32)


def backward_product(grad_rows, weight):
    return jnp.einsum("tb,ab->ta", grad_rows, weight, preferred_element_type=jnp.float32)


def block_scores(query_rows, key_rows, key_mask, score_scale):
    raw_scores = (
        jnp.einsum("qhd,khd->hqk", query_rows, key_rows, preferred_element_type=jnp.float32)
        * score_scale
    )
    return jnp.where(key_mask[None], raw_scores, -1e30)


def body(
    query_tokens,
    passage_tokens,
    query_lengths,
    passage_lengths,
    positives,
    w_query,
    b_query,
    w_key,
    w_value,
    b_value,
    w_out,
    b_out,
    norm1_gain,
    norm1_bias,
    w_in,
    b_in,
    w_down,
    b_down,
    norm2_gain,
    norm2_bias,
    query_out_grad,
    passage_out_grad,
):
    model_width = query_tokens.shape[1]
    head_size = model_width // HEADS
    score_scale = head_size ** (-0.5)

    def tower_forward(rows_in, lengths, seg_len):
        row_count = rows_in.shape[0]
        block_rows = min(row_count, PASS_LEN)
        block_count = row_count // block_rows
        position = jnp.arange(row_count, dtype=jnp.int32)
        len_tok = jnp.repeat(lengths, seg_len)
        key_valid = position % seg_len < len_tok
        valid_blocks = key_valid.reshape(block_count, block_rows)
        matching_pair_index = jnp.arange(block_rows, dtype=jnp.int32)
        same_seq = (
            matching_pair_index[:, None] // seg_len == matching_pair_index[None, :] // seg_len
        )

        def split_heads(rows):
            return rows.reshape(block_count, block_rows, HEADS, head_size)

        query_b = (right_mul(rows_in, w_query) + b_query).astype(jnp.bfloat16)
        key_b = right_mul(rows_in, w_key).astype(jnp.bfloat16)
        value_b = (right_mul(rows_in, w_value) + b_value).astype(jnp.bfloat16)

        def attend(block_items):
            query_rows, key_rows, value_rows, valid_keys = block_items
            scores = block_scores(query_rows, key_rows, same_seq & valid_keys[None, :], score_scale)
            row_top = jnp.max(scores, axis=-1, keepdims=True)
            exp_scores = jnp.exp(scores - row_top)
            row_total = jnp.sum(exp_scores, axis=-1, keepdims=True)
            attn_prob = (exp_scores / row_total).astype(jnp.bfloat16)
            mixed = jnp.einsum(
                "hqk,khd->qhd", attn_prob, value_rows, preferred_element_type=jnp.float32
            )
            return (mixed, (row_top + jnp.log(row_total))[:, :, 0])

        mixed_blocks, log_totals = lax.map(
            attend, (split_heads(query_b), split_heads(key_b), split_heads(value_b), valid_blocks)
        )
        mixed_b = mixed_blocks.reshape(row_count, model_width).astype(jnp.bfloat16)
        resid_one = rows_in.astype(jnp.float32) + right_mul(mixed_b, w_out) + b_out
        hidden_one, back_norm_one = jax.vjp(layer_norm, resid_one, norm1_gain, norm1_bias)
        hidden_one_b = hidden_one.astype(jnp.bfloat16)
        pre_act = right_mul(hidden_one_b, w_in) + b_in
        act_value, back_gelu = jax.vjp(gelu_exact, pre_act)
        act_b = act_value.astype(jnp.bfloat16)
        resid_two = hidden_one + right_mul(act_b, w_down) + b_down
        layer_out, back_norm_two = jax.vjp(layer_norm, resid_two, norm2_gain, norm2_bias)
        seq_slots = jnp.arange(lengths.shape[0], dtype=jnp.int32)
        member = ((position[None, :] // seg_len == seq_slots[:, None]) & key_valid[None, :]).astype(
            jnp.float32
        )
        member = member / lengths[:, None].astype(jnp.float32)
        pooled_rows = jnp.dot(member, layer_out, precision=lax.Precision.HIGHEST)
        unit_value, back_unit = jax.vjp(unit_rows, pooled_rows)
        return {
            "rows_in": rows_in,
            "query_b": query_b,
            "key_b": key_b,
            "value_b": value_b,
            "valid_blocks": valid_blocks,
            "same_seq": same_seq,
            "log_totals": log_totals,
            "mixed_b": mixed_b,
            "back_norm_one": back_norm_one,
            "hidden_one_b": hidden_one_b,
            "back_gelu": back_gelu,
            "act_b": act_b,
            "back_norm_two": back_norm_two,
            "layer_out": layer_out,
            "member": member,
            "unit_value": unit_value,
            "back_unit": back_unit,
            "split_heads": split_heads,
            "row_count": row_count,
        }

    def backward_ffn(saved, out_grad_rows, grad_unit):
        grad_pool = saved["back_unit"](grad_unit)[0]
        grad_layer = out_grad_rows.astype(jnp.float32) + jnp.dot(
            saved["member"].T, grad_pool, precision=lax.Precision.HIGHEST
        )
        grad_resid_two, second_norm_gain_gradient, grad_bias_two = saved["back_norm_two"](
            grad_layer
        )
        grad_branch_b = grad_resid_two.astype(jnp.bfloat16)
        grad_b_down = jnp.sum(grad_branch_b.astype(jnp.float32), axis=0)
        grad_w_down = weight_grad(saved["act_b"], grad_branch_b)
        grad_pre_b = saved["back_gelu"](backward_product(grad_branch_b, w_down))[0].astype(
            jnp.bfloat16
        )
        grad_b_in = jnp.sum(grad_pre_b.astype(jnp.float32), axis=0)
        grad_w_in = weight_grad(saved["hidden_one_b"], grad_pre_b)
        grad_hidden_one = grad_resid_two + backward_product(grad_pre_b, w_in)
        return (
            grad_hidden_one,
            (
                grad_w_in,
                grad_b_in,
                grad_w_down,
                grad_b_down,
                second_norm_gain_gradient,
                grad_bias_two,
            ),
        )

    def backward_attn(saved, grad_hidden_one):
        split_heads = saved["split_heads"]
        same_seq = saved["same_seq"]
        row_count = saved["row_count"]
        grad_resid_one, grad_gain_one, grad_bias_one = saved["back_norm_one"](grad_hidden_one)
        grad_attn_b = grad_resid_one.astype(jnp.bfloat16)
        grad_b_out = jnp.sum(grad_attn_b.astype(jnp.float32), axis=0)
        grad_w_out = weight_grad(saved["mixed_b"], grad_attn_b)
        grad_mixed_b = backward_product(grad_attn_b, w_out).astype(jnp.bfloat16)

        def attend_back(block_items):
            query_rows, key_rows, value_rows, valid_keys, log_total, grad_rows = block_items
            scores = block_scores(query_rows, key_rows, same_seq & valid_keys[None, :], score_scale)
            attn_prob = jnp.exp(scores - log_total[:, :, None])
            grad_prob = jnp.einsum(
                "qhd,khd->hqk", grad_rows, value_rows, preferred_element_type=jnp.float32
            )
            grad_value = jnp.einsum(
                "hqk,qhd->khd",
                attn_prob.astype(jnp.bfloat16),
                grad_rows,
                preferred_element_type=jnp.float32,
            )
            row_delta = jnp.sum(grad_prob * attn_prob, axis=-1, keepdims=True)
            grad_score_b = (attn_prob * (grad_prob - row_delta)).astype(jnp.bfloat16)
            grad_query = (
                jnp.einsum(
                    "hqk,khd->qhd", grad_score_b, key_rows, preferred_element_type=jnp.float32
                )
                * score_scale
            )
            grad_key = (
                jnp.einsum(
                    "hqk,qhd->khd", grad_score_b, query_rows, preferred_element_type=jnp.float32
                )
                * score_scale
            )
            return (grad_query, grad_key, grad_value)

        grad_query_blk, grad_key_blk, grad_value_blk = lax.map(
            attend_back,
            (
                split_heads(saved["query_b"]),
                split_heads(saved["key_b"]),
                split_heads(saved["value_b"]),
                saved["valid_blocks"],
                saved["log_totals"],
                split_heads(grad_mixed_b),
            ),
        )
        grad_query_b = grad_query_blk.reshape(row_count, model_width).astype(jnp.bfloat16)
        grad_key_b = grad_key_blk.reshape(row_count, model_width).astype(jnp.bfloat16)
        grad_value_b = grad_value_blk.reshape(row_count, model_width).astype(jnp.bfloat16)
        rows_in = saved["rows_in"]
        grad_b_query = jnp.sum(grad_query_b.astype(jnp.float32), axis=0)
        grad_b_value = jnp.sum(grad_value_b.astype(jnp.float32), axis=0)
        grad_w_query = weight_grad(rows_in, grad_query_b)
        grad_w_key = weight_grad(rows_in, grad_key_b)
        grad_w_value = weight_grad(rows_in, grad_value_b)
        input_grad = (
            grad_resid_one
            + backward_product(grad_query_b, w_query)
            + backward_product(grad_key_b, w_key)
            + backward_product(grad_value_b, w_value)
        )
        return (
            input_grad,
            (
                grad_w_query,
                grad_b_query,
                grad_w_key,
                grad_w_value,
                grad_b_value,
                grad_w_out,
                grad_b_out,
                grad_gain_one,
                grad_bias_one,
            ),
        )

    question_retained = tower_forward(query_tokens, query_lengths, QRY_LEN)
    passage_saved = tower_forward(passage_tokens, passage_lengths, PASS_LEN)
    unit_query_b = question_retained["unit_value"].astype(jnp.bfloat16)
    unit_passage_b = passage_saved["unit_value"].astype(jnp.bfloat16)
    query_count = query_lengths.shape[0]
    passage_count = passage_lengths.shape[0]
    device_count = lax.axis_size(("stream", "batch"))
    my_index = lax.axis_index(("stream", "batch"))
    query_start = my_index * query_count
    passage_total = passage_count * device_count
    passage_slots = jnp.arange(passage_total, dtype=jnp.int32)
    passage_all = lax.all_gather(unit_passage_b, ("stream", "batch"), axis=0, tiled=True)
    my_positives = lax.dynamic_slice_in_dim(positives, query_start, query_count, 0)
    angular_match_matrix = jnp.einsum(
        "qd,pd->qp", unit_query_b, passage_all, preferred_element_type=jnp.float32
    )
    scaled_match_scores = angular_match_matrix / sharpness_divisor
    logit_top = jnp.max(scaled_match_scores, axis=-1, keepdims=True)
    normalizer_logsum_value = logit_top + jnp.log(
        jnp.sum(jnp.exp(scaled_match_scores - logit_top), axis=-1, keepdims=True)
    )
    chosen_match_entry = (my_positives[:, None] == passage_slots[None, :]).astype(jnp.float32)
    loss_local = jnp.sum(
        normalizer_logsum_value[:, 0] - jnp.sum(scaled_match_scores * chosen_match_entry, axis=-1)
    )
    cosine_gradient = (
        (jnp.exp(scaled_match_scores - normalizer_logsum_value) - chosen_match_entry)
        / sharpness_divisor
    ).astype(jnp.bfloat16)
    grad_unit_query = right_mul(cosine_gradient, passage_all)
    passage_part = weight_grad(cosine_gradient, unit_query_b)
    grad_unit_passage = lax.psum_scatter(
        passage_part, ("stream", "batch"), scatter_dimension=0, tiled=True
    )
    hidden_query, ffn_query = backward_ffn(question_retained, query_out_grad, grad_unit_query)
    hidden_passage, ffn_passage = backward_ffn(passage_saved, passage_out_grad, grad_unit_passage)
    ffn_grads = jax.tree.map(jnp.add, ffn_query, ffn_passage)
    query_input_grad, attn_query = backward_attn(question_retained, hidden_query)
    passage_input_grad, attn_passage = backward_attn(passage_saved, hidden_passage)
    attn_local = jax.tree.map(jnp.add, attn_query, attn_passage)
    summed_grads = lax.psum(
        (
            attn_local[0],
            attn_local[1],
            attn_local[2],
            attn_local[3],
            attn_local[4],
            attn_local[5],
            attn_local[6],
            attn_local[7],
            attn_local[8],
            loss_local,
            ffn_grads[0],
            ffn_grads[1],
            ffn_grads[2],
            ffn_grads[3],
            ffn_grads[4],
            ffn_grads[5],
        ),
        ("stream", "batch"),
    )
    attn_grads = summed_grads[:10]
    ffn_grads = summed_grads[10:]
    loss = attn_grads[9] / (query_count * device_count)
    return (
        question_retained["layer_out"].astype(jnp.bfloat16),
        passage_saved["layer_out"].astype(jnp.bfloat16),
        query_input_grad,
        passage_input_grad,
        loss,
        attn_grads[0],
        attn_grads[1],
        attn_grads[2],
        attn_grads[3],
        attn_grads[4],
        attn_grads[5],
        attn_grads[6],
        attn_grads[7],
        attn_grads[8],
        ffn_grads[0],
        ffn_grads[1],
        ffn_grads[2],
        ffn_grads[3],
        ffn_grads[4],
        ffn_grads[5],
    )


def solution(mesh):
    placed = (
        P(("stream", "batch"), None),
        P(("stream", "batch"), None),
        P(("stream", "batch")),
        P(("stream", "batch")),
        P(),
        P(),
        P(),
        P(),
        P(),
        P(),
        P(),
        P(),
        P(),
        P(),
        P(),
        P(),
        P(),
        P(),
        P(),
        P(),
        P(("stream", "batch"), None),
        P(("stream", "batch"), None),
    )
    return jax.shard_map(
        body,
        mesh=mesh,
        in_specs=placed,
        out_specs=(
            P(("stream", "batch"), None),
            P(("stream", "batch"), None),
            P(("stream", "batch"), None),
            P(("stream", "batch"), None),
            P(),
            P(),
            P(),
            P(),
            P(),
            P(),
            P(),
            P(),
            P(),
            P(),
            P(),
            P(),
            P(),
            P(),
            P(),
            P(),
        ),
        check_vma=False,
    )
```

profile of v0, /device:TPU:0, one launch (start us, length us, event | category | flops | bytes accessed | tf_op | source)
XLA Modules:
  0.0 934.7 jit_solution(5709258584635342977)
XLA Ops:
  12.3 4.5 add_convert_fusion.1
  17.1 2.5 add_convert_fusion.2
  20.6 2.5 convolution_convert_fusion.1
  31.6 2.4 reshape.609
  35.7 2.6 copy.125
  38.3 3.8 reshape.608
  42.1 2.9 copy.128
  45.0 2.6 copy.127
  47.6 3.8 reshape.610
  51.4 2.9 copy.130
  55.6 23.3 %while.6 = (s32[]{:T(128)}, bf16[2,512,12,64]{1,3,2,0:T(8,128)(2,1)}, f32[2,12,512]{2,1,0:T(8,128)S(1)}, bf16[2,512,12,64]{1,3,2,0:T(8,128)(2,1)}, pred[2,512]{1...) while((s32[]{:T(128)}, ...), condition=%wide.region_9.10_spmd.clone, body=%wide.region_6.9_spmd.clone.sunk | while | flops 843573248 | bytes 42956396 | solution.py:109
  55.9 3.2 fusion.243
  59.1 2.6 fusion.244
  61.7 5.5 bitcast_dynamic-update-slice_fusion.10
  67.4 3.2 fusion.243
  70.7 2.6 fusion.244
  73.2 5.5 bitcast_dynamic-update-slice_fusion.10
  79.0 3.6 copy.131
  87.5 6.1 multiply_convert_fusion.2
  95.4 36.3 %multiply_convert_fusion.1 = (bf16[1024,3072]{1,0:T(8,128)(2,1)}, f32[1024,3072]{1,0:T(8,128)}, f32[1024,3072]{1,0:T(8,128)}) fusion(f32[3072]{0:T(1024)S(1)} %copy-done.107, bf16[768,3072]{1,0:T(8,128)(2,1)S(1)} %bitcast.241, f32[1024,768]{0,1:T(8,128)S(1)} %get-tuple-element.451, f32[768]{0:T(1024)S(1)} %copy-done.77, f32[768]{0:T(1024)S(1)} %copy-done.64, ...), kind=kOutput, calls=%fused_computation.62 | convolution fusion | flops 5043388416 | bytes 39348224 | tf_op jit(solution)/shard_map/dot_general | solution.py:30
  131.7 7.8 fusion.139
  141.2 3.0 multiply_reduce_fusion.16
  144.3 43.5 %all-gather = bf16[32,2,768]{2,1,0:T(2,128)(2,1)S(1)} all-gather(bf16[1,2,768]{2,1,0:T(2,128)(2,1)S(1)} %fusion.108), channel_id=1, replica_groups=mesh['stream'=2,'batch'=16] {'stream','batch'}, dimensions={0}, use_global_device_ids=true | all-gather | bytes 101376 | tf_op jit(solution)/shard_map/all_gather | solution.py:270
  193.5 4.9 convert_reduce_fusion.5
  198.4 2.4 multiply_reduce_fusion.9
  210.2 99.5 %all-reduce.6.cloned.1.call-done = f32[64,768]{1,0:T(8,128)} async-done(((f32[64,768]{1,0:T(8,128)}), f32[64,768]{1,0:T(8,128)}) %all-reduce.6.cloned.1.call-update) | async-done | bytes 196624
  310.6 6.6 multiply_reduce_fusion.1
  317.1 2.5 fusion.130
  321.4 17.6 %convert_reduce_fusion = (f32[3072]{0:T(1024)}, bf16[1024,3072]{1,0:T(8,128)(2,1)}) fusion(f32[1024,3072]{1,0:T(8,128)} %get-tuple-element.434, bf16[1024,768]{0,1:T(8,128)(2,1)S(1)} %get-tuple-element.414, bf16[3072,768]{1,0:T(8,128)(2,1)} %param.42, f32[1024,3072]{1,0:T(8,128)} %get-tuple-element.452, f32[3072]{0:T(1024)S(1)} %copy-done.107), kind=kOutput, calls=%fused_computation.60 | convolution fusion | flops 4885312512 | bytes 37773312 | tf_op jit(solution)/shard_map/tb,ab->ta/dot_general | solution.py:38
  339.0 11.2 %multiply_reduce_fusion.2 = (f32[768]{0:T(1024)}, f32[1024]{0:T(1024)S(1)}, f32[768]{0:T(1024)}, f32[1024,768]{0,1:T(8,128)S(1)}) fusion(f32[1024,768]{0,1:T(8,128)S(1)} %copy-done.17, f32[1024]{0:T(1024)S(1)} %fusion.102, f32[1024]{0:T(1024)S(1)} %broadcast_multiply_fusion.1, f32[768]{0:T(1024)S(1)} %copy-done.64, ...), kind=kOutput, calls=%fused_computation.83 | convolution fusion | flops 4839699456 | bytes 20472832 | tf_op jit(solution)/shard_map/tb,ab->ta/dot_general | solution.py:38
  350.2 5.3 fusion.125
  360.3 2.6 convolution_convert_fusion
  363.0 8.1 fusion.145
  371.1 5.3 convolution_add_fusion.1
  379.9 2.4 reshape.612
  382.3 2.9 copy.142
  389.1 51.7 %while.7 = (s32[]{:T(128)}, bf16[2,512,12,64]{1,3,2,0:T(8,128)(2,1)}, bf16[2,512,12,64]{1,3,2,0:T(8,128)(2,1)}, bf16[2,512,12,64]{1,3,2,0:T(8,128)(2,1)}, bf16[2...) while((s32[]{:T(128)}, ...), condition=%wide.region_32.33_spmd.clone, body=%wide.region_30.32_spmd.clone.sunk | while | flops 2061756416 | bytes 149881680 | solution.py:218
  389.6 3.1 fusion.253
  392.7 3.9 bitcast_dynamic-update-slice_fusion.14
  396.7 6.9 multiply_reduce_fusion.19
  403.5 7.1 multiply_convert_fusion.12
  410.6 2.0 bitcast_dynamic-update-slice_fusion.13
  415.3 3.1 fusion.253
  418.4 4.0 bitcast_dynamic-update-slice_fusion.14
  422.4 6.9 multiply_reduce_fusion.19
  429.2 7.1 multiply_convert_fusion.12
  436.3 2.0 bitcast_dynamic-update-slice_fusion.13
  440.9 3.1 copy.146
  446.5 3.6 copy.148
  455.3 5.2 convolution_add_fusion
  464.2 2.1 add_bitcast_fusion.1
  467.3 2.0 convolution_add_fusion.6
  472.6 2.4 convert_reduce_fusion.3
  475.4 44.4 %all-reduce.1 = (f32[]{:T(128)}, f32[768]{0:T(1024)}, f32[768]{0:T(1024)}, f32[768]{0:T(1024)}, f32[768]{0:T(1024)}, /*index=5*/f32[768]{0:T(1024)}, f32[3072]{0...) all-reduce(f32[]{:T(128)} %get-tuple-element.423, ...), channel_id=1, replica_groups=mesh['stream'=2,'batch'=16] {'stream','batch'}, use_global_device_ids=true, to_apply=%region_35.36 | all-reduce | flops 9217 | bytes 73736 | tf_op jit(solution)/shard_map/psum | solution.py:299
  519.8 2.6 copy.150
  522.4 3.0 fusion.146
  527.9 3.2 add_add_fusion.2
  531.1 3.6 copy.151
  535.3 368.2 %all-reduce.8.cloned.1.call-done = (f32[768,768]{0,1:T(8,128)}, f32[768,768]{0,1:T(8,128)}, f32[768,768]{0,1:T(8,128)}, f32[768,768]{1,0:T(8,128)}, f32[768,3072]{1,0:T(8,128)}, /*index=5*/f32[3072,768]{1,0:T(8,128)}) async-done(((f32[768,768]{0,1:T(8,128)}, f32[768,768]{0,1:T(8,128)}, f32[768,768]{0,1:T(8,128)}, f32[768,768]{1,0:T(8,128)}, f32[768,3072]{1,0:T(8,128)}, /*index=5*/f32[3072,768]{1,0:T(8,128)}), ...) | async-done | bytes 28311568 | tf_op jit(solution)/shard_map/psum | solution.py:299
  903.6 3.2 copy.152
  906.8 1.9 copy.153
  908.7 3.2 copy.154
  913.3 9.3 copy.209
  922.7 3.7 copy.210
  (406 shorter events, 80.5 us)
Async XLA Ops:
  7.2 21.4 %copy-start = (bf16[768,768]{1,0:T(8,128)(2,1)S(1)}, bf16[768,768]{1,0:T(8,128)(2,1)}, u32[]{:S(2)}) copy-start(bf16[768,768]{1,0:T(8,128)(2,1)} %param.36) | copy-start | bytes 3538948
  7.2 302.5 %all-reduce.6.cloned.1.call-start = ((), (), s32[]{:S(2)}) async-start(), calls=%async_computation | async-start | bytes 393216
  7.3 20.4 %copy-start.97 = (s32[128]{0:T(128)}, s32[128]{0:T(128)S(1)}, u32[]{:S(2)}) copy-start(s32[128]{0:T(128)S(1)} %and_select_fusion.2) | copy-start | bytes 1540
  12.2 4.5 copy-start.19
  12.2 4.5 copy-start.21
  12.2 4.5 copy-start.89
  12.2 4.8 copy-start.45
  78.9 4.1 copy-start.2
  78.9 4.1 copy-start.53
  79.0 4.1 copy-start.60
  79.0 4.1 copy-start.62
  79.0 4.1 copy-start.49
  83.1 10.5 %slice-start.6 = ((s8[4718592]{0:T(1024)(128)(4,1)}), s8[4194304]{0:T(1024)(128)(4,1)S(1)}, s32[]{:S(2)}) async-start(s8[4718592]{0:T(1024)(128)(4,1)} %bitcast.238), calls=%async_computation.8 | async-start | bytes 8388608
  84.8 46.9 %copy-start.16 = (f32[1024,768]{0,1:T(8,128)}, f32[1024,768]{0,1:T(8,128)S(1)}, u32[]{:S(2)}) copy-start(f32[1024,768]{0,1:T(8,128)S(1)} %get-tuple-element.451) | copy-start | bytes 9437188
  85.3 8.3 copy-start.70
  87.5 6.1 slice-start.7
  87.5 6.1 copy-start.91
  139.6 48.3 %copy-start.109 = (s32[64]{0:T(128)S(1)}, s32[64]{0:T(128)}, u32[]{:S(2)}) copy-start(s32[64]{0:T(128)} %param.30) | copy-start | bytes 772
  139.6 50.6 %copy-start.66 = (f32[12,128]{1,0:T(8,128)S(1)}, f32[12,128]{1,0:T(8,128)}, u32[]{:S(2)}) copy-start(f32[12,128]{1,0:T(8,128)} %copy-done.65) | copy-start | bytes 18436
  139.6 50.6 %copy-start.75 = (f32[12,128]{1,0:T(8,128)S(1)}, f32[12,128]{1,0:T(8,128)}, u32[]{:S(2)}) copy-start(f32[12,128]{1,0:T(8,128)} %copy-done.74) | copy-start | bytes 18436
  139.6 50.9 %copy-start.106 = (bf16[128,768]{1,0:T(8,128)(2,1)S(1)}, bf16[128,768]{1,0:T(8,128)(2,1)}, u32[]{:S(2)}) copy-start(bf16[128,768]{1,0:T(8,128)(2,1)} %param.46) | copy-start | bytes 589828
  141.2 57.2 %slice-start.10 = ((s8[4718592]{0:T(1024)(128)(4,1)}), s8[524288]{0:T(1024)(128)(4,1)S(1)}, s32[]{:S(2)}) async-start(s8[4718592]{0:T(1024)(128)(4,1)} %bitcast.242), calls=%async_computation.12 | async-start | bytes 1048576
  190.1 713.5 %all-reduce.8.cloned.1.call-start = ((), (), s32[]{:S(2)}) async-start(), calls=%async_computation.1 | async-start | bytes 56623104 | tf_op jit(solution)/shard_map/psum | solution.py:299
  193.5 4.9 copy-start.55
  193.5 4.9 slice-start.11
  201.1 4.6 copy-start.30
  201.1 4.6 copy-start.99
  202.5 4.2 copy-start.44
  310.6 6.6 copy-start.8
  321.4 17.6 %copy-start.17 = (f32[1024,768]{0,1:T(8,128)S(1)}, f32[1024,768]{0,1:T(8,128)}, u32[]{:S(2)}) copy-start(f32[1024,768]{0,1:T(8,128)} %copy-done.16) | copy-start | bytes 9437188
  339.0 11.2 %copy-start.113 = (bf16[1024,3072]{1,0:T(8,128)(2,1)S(1)}, bf16[1024,3072]{1,0:T(8,128)(2,1)}, u32[]{:S(2)}) copy-start(bf16[1024,3072]{1,0:T(8,128)(2,1)} %get-tuple-element.474) | copy-start | bytes 18874372
  350.2 5.3 copy-start.71
  356.3 4.0 copy-start.5
  356.3 4.0 copy-start.68
  358.9 4.1 slice-start.12
  362.9 8.1 copy-start.35
  371.1 5.3 copy-start.58
  403.5 7.1 copy-start.25
  418.4 4.0 copy-start.11
  429.2 7.1 copy-start.25
  444.5 9.0 copy-start.50
  446.5 5.5 copy-start.52
  446.5 4.1 copy-start.46
  450.6 4.3 slice-start.3
  455.3 5.2 copy-start.22
  455.3 5.2 copy-start.38
  471.2 4.0 copy-start.81
  471.2 4.0 copy-start.93
  471.2 4.0 copy-start.80
  471.2 4.0 copy-start.92
  471.2 4.0 copy-start.78
  471.2 4.0 copy-start.82
  471.2 4.0 copy-start.87
  471.3 4.0 copy-start.88
  471.3 4.0 copy-start.86
  471.3 4.0 copy-start.95
  471.3 4.0 copy-start.85
  471.3 4.0 copy-start.94
  471.3 4.0 copy-start.79
  471.3 4.0 copy-start.83
  475.0 47.4 %copy-start.27 = (bf16[768,768]{1,0:T(8,128)(2,1)S(1)}, bf16[768,768]{1,0:T(8,128)(2,1)}, u32[]{:S(2)}) copy-start(bf16[768,768]{1,0:T(8,128)(2,1)} %param.31) | copy-start | bytes 3538948
  911.9 10.7 %slice-start = ((s8[9437184]{0:T(1024)(128)(4,1)}), s8[4194304]{0:T(1024)(128)(4,1)S(1)}, s32[]{:S(2)}) async-start(s8[9437184]{0:T(1024)(128)(4,1)} %bitcast.228), calls=%async_computation.2 | async-start | bytes 8388608
  913.3 9.3 slice-start.1
  913.3 9.3 slice-start.2
  (73 other events, 165.8 us)
Sparse Core Ops, SparseCore 0:
  190.2 119.4 all-reduce.5
  466.5 437.0 all-reduce.7
where the time goes:
time: 939 us; the launch traced here: 935 us
  waiting for transfers between devices  468 us (50%)
  matrix products  225 us (24%)
  local copies, waits for them, and re-layouts  97 us (10%)
  blocking collectives  87.9 us (9%)
  other arithmetic  37.9 us (4%)
  between operations  17.8 us (2%)
    psum x1, waiting for transfers between devices, body(): lax.psum((attn_local[0], attn_local[1], attn_local[2], attn_local[3], att...  368 us
    unnamed x3, waiting for transfers between devices  99.6 us
    dot_general x13, matrix products, right_mul(): return jnp.dot(left, weight, preferred_element_type=jnp.float32)  66 us
    unnamed x263, local copies, waits for them, and re-layouts  54.3 us
    dot_general x12, matrix products, backward_product(): jnp.einsum('tb,ab->ta', grad_rows, weight, preferred_element_type=jnp.flo...  51.9 us
    psum x1, blocking collectives, body(): lax.psum((attn_local[0], attn_local[1], attn_local[2], attn_local[3], att...  44.4 us
    all_gather x1, blocking collectives, body(): lax.all_gather(unit_passage_b, ('stream', 'batch'), axis=0, tiled=True)  43.5 us
    dot_general x13, matrix products, weight_grad(): jnp.einsum('ta,tb->ab', left, right, preferred_element_type=jnp.float32)  38.1 us
  transfers between devices with their start and end apart: 2, of which 2 were waited for; matrix products, arithmetic and copies ran while one was open for 4% of the time, Pallas kernels for 0%

commit v1 on v0

--- a/solution.py
+++ b/solution.py
@@ -44,6 +44,71 @@
         * score_scale
     )
     return jnp.where(key_mask[None], raw_scores, -1e30)
+
+
+AXES = ("stream", "batch")
+
+
+def swap_with(value, mask, device_count):
+    return lax.ppermute(value, AXES, [(i, i ^ mask) for i in range(device_count)])
+
+
+def bit_orders(device_count):
+    top = device_count // 2
+    rest = []
+    mask = 4
+    while mask < top:
+        rest.append(mask)
+        mask *= 2
+    return ([1, top, 2] + rest, [1, 2, top] + rest)
+
+
+def gather_relative(value, device_count):
+    top = device_count // 2
+    groups = [[1], [2, top]]
+    rest = []
+    mask = 4
+    while mask < top:
+        rest.append(mask)
+        mask *= 2
+    while rest:
+        groups.append(rest[:2])
+        rest = rest[2:]
+    relative = [0]
+    for group in groups:
+        combos = [0]
+        for mask in group:
+            combos = combos + [c ^ mask for c in combos]
+        got = [value] + [swap_with(value, c, device_count) for c in combos[1:]]
+        value = jnp.concatenate(got, axis=0)
+        relative = [c ^ r for c in combos for r in relative]
+    return value, relative
+
+
+def scatter_sum(part, masks, my_index, device_count):
+    for mask in masks:
+        half = part.shape[0] // 2
+        bit = ((my_index & mask) != 0).astype(jnp.int32)
+        send = lax.dynamic_slice_in_dim(part, (1 - bit) * half, half, 0)
+        keep = lax.dynamic_slice_in_dim(part, bit * half, half, 0)
+        got = swap_with(send, mask, device_count)
+        part = (keep.astype(jnp.float32) + got.astype(jnp.float32)).astype(part.dtype)
+    return part
+
+
+def gather_back(part, masks, my_index, device_count):
+    for mask in reversed(masks):
+        bit = (my_index & mask) != 0
+        got = swap_with(part, mask, device_count)
+        part = jnp.where(
+            bit, jnp.concatenate([got, part], 0), jnp.concatenate([part, got], 0)
+        )
+    return part
+
+
+def sum_all(part, masks, my_index, device_count):
+    part = scatter_sum(part, masks, my_index, device_count)
+    return gather_back(part, masks, my_index, device_count)
 
 
 def body(
@@ -262,64 +327,96 @@
     unit_passage_b = passage_saved["unit_value"].astype(jnp.bfloat16)
     query_count = query_lengths.shape[0]
     passage_count = passage_lengths.shape[0]
-    device_count = lax.axis_size(("stream", "batch"))
-    my_index = lax.axis_index(("stream", "batch"))
-    query_start = my_index * query_count
-    passage_total = passage_count * device_count
-    passage_slots = jnp.arange(passage_total, dtype=jnp.int32)
-    passage_all = lax.all_gather(unit_passage_b, ("stream", "batch"), axis=0, tiled=True)
-    my_positives = lax.dynamic_slice_in_dim(positives, query_start, query_count, 0)
-    angular_match_matrix = jnp.einsum(
-        "qd,pd->qp", unit_query_b, passage_all, preferred_element_type=jnp.float32
-    )
-    scaled_match_scores = angular_match_matrix / sharpness_divisor
+    device_count = lax.axis_size(AXES)
+    my_index = lax.axis_index(AXES)
+    units, relative = gather_relative(
+        jnp.concatenate([unit_query_b, unit_passage_b], 0)[None], device_count
+    )
+    query_all = units[:, :query_count].reshape(device_count * query_count, model_width)
+    passage_all = units[:, query_count:].reshape(device_count * passage_count, model_width)
+    owner = jnp.array(relative, jnp.int32) ^ my_index
+    query_ids = (owner[:, None] * query_count + jnp.arange(query_count)[None, :]).reshape(-1)
+    passage_ids = (owner[:, None] * passage_count + jnp.arange(passage_count)[None, :]).reshape(-1)
+    scaled_match_scores = (
+        jnp.einsum("qd,pd->qp", query_all, passage_all, preferred_element_type=jnp.float32)
+        / sharpness_divisor
+    )
     logit_top = jnp.max(scaled_match_scores, axis=-1, keepdims=True)
     normalizer_logsum_value = logit_top + jnp.log(
         jnp.sum(jnp.exp(scaled_match_scores - logit_top), axis=-1, keepdims=True)
     )
-    chosen_match_entry = (my_positives[:, None] == passage_slots[None, :]).astype(jnp.float32)
-    loss_local = jnp.sum(
+    chosen_match_entry = (positives[query_ids][:, None] == passage_ids[None, :]).astype(jnp.float32)
+    loss_sum = jnp.sum(
         normalizer_logsum_value[:, 0] - jnp.sum(scaled_match_scores * chosen_match_entry, axis=-1)
     )
     cosine_gradient = (
         (jnp.exp(scaled_match_scores - normalizer_logsum_value) - chosen_match_entry)
         / sharpness_divisor
     ).astype(jnp.bfloat16)
-    grad_unit_query = right_mul(cosine_gradient, passage_all)
-    passage_part = weight_grad(cosine_gradient, unit_query_b)
-    grad_unit_passage = lax.psum_scatter(
-        passage_part, ("stream", "batch"), scatter_dimension=0, tiled=True
-    )
+    grad_unit_query = right_mul(cosine_gradient[:query_count], passage_all)
+    grad_unit_passage = weight_grad(cosine_gradient[:, :passage_count], query_all)
     hidden_query, ffn_query = backward_ffn(question_retained, query_out_grad, grad_unit_query)
     hidden_passage, ffn_passage = backward_ffn(passage_saved, passage_out_grad, grad_unit_passage)
     ffn_grads = jax.tree.map(jnp.add, ffn_query, ffn_passage)
     query_input_grad, attn_query = backward_attn(question_retained, hidden_query)
     passage_input_grad, attn_passage = backward_attn(passage_saved, hidden_passage)
     attn_local = jax.tree.map(jnp.add, attn_query, attn_passage)
-    summed_grads = lax.psum(
-        (
-            attn_local[0],
-            attn_local[1],
-            attn_local[2],
-            attn_local[3],
-            attn_local[4],
-            attn_local[5],
-            attn_local[6],
-            attn_local[7],
-            attn_local[8],
-            loss_local,
-            ffn_grads[0],
-            ffn_grads[1],
-            ffn_grads[2],
-            ffn_grads[3],
-            ffn_grads[4],
-            ffn_grads[5],
-        ),
-        ("stream", "batch"),
-    )
-    attn_grads = summed_grads[:10]
-    ffn_grads = summed_grads[10:]
-    loss = attn_grads[9] / (query_count * device_count)
+    order_x, order_y = bit_orders(device_count)
+
+    def reduce_pair(first, second):
+        return (
+            sum_all(first.astype(jnp.bfloat16), order_x, my_index, device_count).astype(jnp.float32),
+            sum_all(second.astype(jnp.bfloat16), order_y, my_index, device_count).astype(jnp.float32),
+        )
+
+    down_half = ffn_grads[2].shape[0] // 2
+    down_top, down_low = reduce_pair(ffn_grads[2][:down_half], ffn_grads[2][down_half:])
+    in_half = ffn_grads[0].shape[1] // 2
+    in_left, in_right = reduce_pair(ffn_grads[0][:, :in_half], ffn_grads[0][:, in_half:])
+    proj_left, proj_right = reduce_pair(
+        jnp.concatenate([attn_local[0], attn_local[2]], 1),
+        jnp.concatenate([attn_local[3], attn_local[5]], 1),
+    )
+    smalls = (
+        attn_local[1],
+        attn_local[4],
+        attn_local[6],
+        attn_local[7],
+        attn_local[8],
+        ffn_grads[1],
+        ffn_grads[3],
+        ffn_grads[4],
+        ffn_grads[5],
+    )
+    packed = jnp.concatenate([v.reshape(-1, model_width) for v in smalls], 0)
+    for mask in order_x:
+        packed = packed + swap_with(packed, mask, device_count)
+    cut = []
+    row = 0
+    for v in smalls:
+        rows = v.shape[0] // model_width
+        cut.append(packed[row : row + rows].reshape(-1))
+        row += rows
+    attn_grads = (
+        proj_left[:, :model_width],
+        cut[0],
+        proj_left[:, model_width:],
+        proj_right[:, :model_width],
+        cut[1],
+        proj_right[:, model_width:],
+        cut[2],
+        cut[3],
+        cut[4],
+    )
+    ffn_grads = (
+        jnp.concatenate([in_left, in_right], 1),
+        cut[5],
+        jnp.concatenate([down_top, down_low], 0),
+        cut[6],
+        cut[7],
+        cut[8],
+    )
+    loss = loss_sum / (query_count * device_count)
     return (
         question_retained["layer_out"].astype(jnp.bfloat16),
         passage_saved["layer_out"].astype(jnp.bfloat16),

time: 939 us -> 612 us (0.65)
  waiting for transfers between devices: 468 us -> 140 us
  blocking collectives: 87.9 us -> 0 us
  starting transfers between devices: 0.08 us -> 69.3 us
  other arithmetic: 37.9 us -> 69.4 us
  between operations: 17.8 us -> 5.5 us
    psum x1 -> x0, waiting for transfers between devices: 368 us -> none  [body(): lax.psum((attn_local[0], attn_local[1], attn_local[2], attn_local[3], att...]
    ppermute x0 -> x72, waiting for transfers between devices: none -> 140 us  [swap_with(): lax.ppermute(value, AXES, [(i, i ^ mask) for i in range(device_count)])]
    unnamed x3 -> x0, waiting for transfers between devices: 99.6 us -> none
    ppermute x0 -> x72, starting transfers between devices: none -> 69.3 us  [swap_with(): lax.ppermute(value, AXES, [(i, i ^ mask) for i in range(device_count)])]
    psum x1 -> x0, blocking collectives: 44.4 us -> none  [body(): lax.psum((attn_local[0], attn_local[1], attn_local[2], attn_local[3], att...]
    all_gather x1 -> x0, blocking collectives: 43.5 us -> none  [body(): lax.all_gather(unit_passage_b, ('stream', 'batch'), axis=0, tiled=True)]
    unnamed x263 -> x305, local copies, waits for them, and re-layouts: 54.3 us -> 35.5 us
    convert_element_type x0 -> x34, other arithmetic: none -> 12.1 us  [the longest x30 10.6 us: scatter_sum(): (keep.astype(jnp.float32) + got.astype(jnp.float32)).astype(part.dtype)]
  transfers between devices with their start and end apart: 2 -> 72, of which waited for: 2 -> 37; matrix products, arithmetic and copies ran while one was open for 4% -> 11% of each run, Pallas kernels for 0% -> 0%
where the time goes in v1:
time: 612 us; the launch traced here: 607 us
  matrix products  228 us (37%)
  waiting for transfers between devices  140 us (23%)
  local copies, waits for them, and re-layouts  94.2 us (15%)
  other arithmetic  69.4 us (11%)
  starting transfers between devices  69.3 us (11%)
    ppermute x72, waiting for transfers between devices, swap_with(): lax.ppermute(value, AXES, [(i, i ^ mask) for i in range(device_count)])  140 us
    ppermute x72, starting transfers between devices, swap_with(): lax.ppermute(value, AXES, [(i, i ^ mask) for i in range(device_count)])  69.3 us
    dot_general x13, matrix products, right_mul(): return jnp.dot(left, weight, preferred_element_type=jnp.float32)  66 us
    dot_general x12, matrix products, backward_product(): jnp.einsum('tb,ab->ta', grad_rows, weight, preferred_element_type=jnp.flo...  52.6 us
    dot_general x13, matrix products, weight_grad(): jnp.einsum('ta,tb->ab', left, right, preferred_element_type=jnp.float32)  42.3 us
    unnamed x305, local copies, waits for them, and re-layouts  35.5 us
    convert_element_type x3, other arithmetic, attend_back(): grad_score_b = (attn_prob * (grad_prob - row_delta)).astype(jnp.bfloat16)  14.4 us
    dot_general x3, matrix products, attend_back(): jnp.einsum('qhd,khd->hqk', grad_rows, value_rows, preferred_element_type=...  13.9 us
  transfers between devices with their start and end apart: 72, of which 37 were waited for; matrix products, arithmetic and copies ran while one was open for 11% of the time, Pallas kernels for 0%

profile of v1, /device:TPU:0, one launch (start us, length us, event | category | flops | bytes accessed | tf_op | source)
XLA Modules:
  0.0 606.7 jit_solution(6354654885750737989)
XLA Ops:
  5.7 4.5 add_convert_fusion.3
  31.7 3.8 reshape.793
  35.6 2.9 copy.185
  41.0 3.8 reshape.795
  44.9 2.9 copy.187
  49.1 23.3 %while.6 = (s32[]{:T(128)}, bf16[2,512,12,64]{1,3,2,0:T(8,128)(2,1)}, f32[2,12,512]{2,1,0:T(8,128)S(1)}, bf16[2,512,12,64]{1,3,2,0:T(8,128)(2,1)}, pred[2,512]{1...) while((s32[]{:T(128)}, ...), condition=%wide.region_9.10_spmd.clone, body=%wide.region_6.9_spmd.clone.sunk | while | flops 843573248 | bytes 42956396 | solution.py:174
  49.3 3.2 fusion.263
  55.1 5.5 bitcast_dynamic-update-slice_fusion.10
  60.9 3.2 fusion.263
  66.7 5.5 bitcast_dynamic-update-slice_fusion.10
  72.4 3.6 copy.188
  81.5 6.1 multiply_convert_fusion.2
  89.4 36.3 %multiply_convert_fusion.1 = (bf16[1024,3072]{1,0:T(8,128)(2,1)}, f32[1024,3072]{1,0:T(8,128)}, f32[1024,3072]{1,0:T(8,128)}) fusion(f32[3072]{0:T(1024)S(1)} %copy-done.135, bf16[768,3072]{1,0:T(8,128)(2,1)S(1)} %bitcast.245, f32[1024,768]{0,1:T(8,128)S(1)} %get-tuple-element.502, f32[768]{0:T(1024)S(1)} %copy-done.101, f32[768]{0:T(1024)S(1)} %copy-done.87, ...), kind=kOutput, calls=%fused_computation.63 | convolution fusion | flops 5043388416 | bytes 39348224 | tf_op jit(solution)/shard_map/dot_general | solution.py:30
  125.8 7.8 %fusion.157 = (f32[1024]{0:T(1024)S(1)}, f32[1024,768]{0,1:T(8,128)S(1)}) fusion(f32[768]{0:T(1024)S(1)} %copy-done.120, bf16[1024,3072]{1,0:T(8,128)(2,1)} %get-tuple-element.464, bf16[3072,768]{1,0:T(8,128)(2,1)S(1)} %bitcast.243, f32[768]{0:T(1024)S(1)} %copy-done.101, f32[768]{0:T(1024)S(1)} %copy-done.87, f32[1024]{0:T(1024)S(1)} %fusion.116, ...), kind=kOutput, calls=%fused_computation.431 | convolution fusion | flops 4837342208 | bytes 17323008 | tf_op jit(solution)/shard_map/dot_general | solution.py:30
  134.4 3.0 multiply_reduce_fusion.16
  138.9 3.9 collective-permute-start.3
  143.4 3.6 collective-permute-done.1
  154.9 5.3 collective-permute-done.5
  166.1 4.9 convert_reduce_fusion.5
  180.6 4.5 multiply_reduce_fusion.1
  189.4 18.7 %convert_reduce_fusion = (f32[3072]{0:T(1024)}, bf16[1024,3072]{1,0:T(8,128)(2,1)}) fusion(f32[1024,3072]{1,0:T(8,128)} %get-tuple-element.465, bf16[1024,768]{0,1:T(8,128)(2,1)S(1)} %get-tuple-element.445, bf16[3072,768]{1,0:T(8,128)(2,1)} %param.43, f32[1024,3072]{1,0:T(8,128)} %get-tuple-element.503, f32[3072]{0:T(1024)S(1)} %copy-done.135), kind=kOutput, calls=%fused_computation.61 | convolution fusion | flops 4885312512 | bytes 37773312 | tf_op jit(solution)/shard_map/tb,ab->ta/dot_general | solution.py:38
  208.1 10.9 %multiply_reduce_fusion.2 = (f32[768]{0:T(1024)}, f32[1024]{0:T(1024)S(1)}, f32[768]{0:T(1024)}, f32[1024,768]{0,1:T(8,128)S(1)}) fusion(f32[1024,768]{0,1:T(8,128)S(1)} %copy-done.20, f32[1024]{0:T(1024)S(1)} %fusion.116, f32[1024]{0:T(1024)S(1)} %broadcast_multiply_fusion.1, f32[768]{0:T(1024)S(1)} %copy-done.87, ...), kind=kOutput, calls=%fused_computation.86 | convolution fusion | flops 4839699456 | bytes 20472832 | tf_op jit(solution)/shard_map/tb,ab->ta/dot_general | solution.py:38
  219.0 7.9 %fusion.138 = f32[768,3072]{1,0:T(8,128)} fusion(bf16[1024,3072]{1,0:T(8,128)(2,1)S(1)} %copy-done.141, f32[1024,768]{0,1:T(8,128)S(1)} %copy-done.20, f32[768]{0:T(1024)S(1)} %copy-done.101, f32[768]{0:T(1024)S(1)} %copy-done.87, f32[1024]{0:T(1024)S(1)} %fusion.116, f32[1024]{0:T(1024)S(1)} %broadcast_multiply_fusion.1), kind=kOutput, calls=%fused_computation.416 | convolution fusion | flops 4835770368 | bytes 18888704 | tf_op jit(solution)/shard_map/ta,tb->ab/dot_general | solution.py:34
  230.4 2.8 fusion.162
  239.9 2.9 copy.199
  246.8 51.6 %while.7 = (s32[]{:T(128)}, bf16[2,512,12,64]{1,3,2,0:T(8,128)(2,1)}, bf16[2,512,12,64]{1,3,2,0:T(8,128)(2,1)}, bf16[2,512,12,64]{1,3,2,0:T(8,128)(2,1)}, bf16[2...) while((s32[]{:T(128)}, ...), condition=%wide.region_31.32_spmd.clone, body=%wide.region_29.31_spmd.clone.sunk | while | flops 2061756416 | bytes 149881680 | solution.py:283
  247.1 3.1 fusion.273
  250.2 3.9 bitcast_dynamic-update-slice_fusion.14
  254.2 6.8 %multiply_reduce_fusion.19 = (f32[12,512]{1,0:T(8,128)S(1)}, f32[12,512,512]{1,2,0:T(8,128)}) fusion(f32[12,512,512]{1,2,0:T(8,128)S(1)} %fusion.273, f32[12,512]{1,0:T(8,128)S(1)} %dynamic-slice_bitcast_fusion.2, pred[512,512]{0,1:T(8,128)(4,1)S(1)} %compare_and_fusion.6, bf16[2,512,12,64]{1,3,2,0:T(8,128)(2,1)S(1)} %copy-done.12, s32[]{:T(128)S(6)} %copy.272, ...), kind=kOutput, calls=%fused_computation.25.clone.1 | convolution fusion | flops 418375680 | bytes 27059200 | tf_op jit(solution)/shard_map/while/body/eval_jaxpr/qhd,khd->hqk/dot_general | solution.py:258
  260.9 7.1 %multiply_convert_fusion.7 = bf16[12,512,512]{1,2,0:T(8,128)(2,1)S(1)} fusion(f32[12,512,512]{1,2,0:T(8,128)} %get-tuple-element.652, f32[12,512,512]{1,2,0:T(8,128)S(1)} %fusion.273, f32[12,512]{1,0:T(8,128)S(1)} %get-tuple-element.653, f32[12,512]{1,0:T(8,128)S(1)} %dynamic-slice_bitcast_fusion.2, pred[512,512]{0,1:T(8,128)(4,1)S(1)} %compare_and_fusion.6), kind=kLoop, calls=%fused_computation.24.clone.1 | loop fusion | flops 18874368 | bytes 31768576 | tf_op jit(solution)/shard_map/while/body/eval_jaxpr/convert_element_type | solution.py:268
  272.7 3.1 fusion.273
  275.8 4.0 bitcast_dynamic-update-slice_fusion.14
  279.8 6.8 %multiply_reduce_fusion.19 = (f32[12,512]{1,0:T(8,128)S(1)}, f32[12,512,512]{1,2,0:T(8,128)}) fusion(f32[12,512,512]{1,2,0:T(8,128)S(1)} %fusion.273, f32[12,512]{1,0:T(8,128)S(1)} %dynamic-slice_bitcast_fusion.2, pred[512,512]{0,1:T(8,128)(4,1)S(1)} %compare_and_fusion.6, bf16[2,512,12,64]{1,3,2,0:T(8,128)(2,1)S(1)} %copy-done.12, s32[]{:T(128)S(6)} %copy.272, ...), kind=kOutput, calls=%fused_computation.25.clone.1 | convolution fusion | flops 418375680 | bytes 27059200 | tf_op jit(solution)/shard_map/while/body/eval_jaxpr/qhd,khd->hqk/dot_general | solution.py:258
  286.6 7.1 %multiply_convert_fusion.7 = bf16[12,512,512]{1,2,0:T(8,128)(2,1)S(1)} fusion(f32[12,512,512]{1,2,0:T(8,128)} %get-tuple-element.652, f32[12,512,512]{1,2,0:T(8,128)S(1)} %fusion.273, f32[12,512]{1,0:T(8,128)S(1)} %get-tuple-element.653, f32[12,512]{1,0:T(8,128)S(1)} %dynamic-slice_bitcast_fusion.2, pred[512,512]{0,1:T(8,128)(4,1)S(1)} %compare_and_fusion.6), kind=kLoop, calls=%fused_computation.24.clone.1 | loop fusion | flops 18874368 | bytes 31768576 | tf_op jit(solution)/shard_map/while/body/eval_jaxpr/convert_element_type | solution.py:268
  300.3 4.2 copy.205
  307.8 2.9 fusion.159
  310.7 3.0 fusion.164
  315.9 2.9 fusion.160
  318.8 3.1 fusion.165
  321.9 7.8 %fusion.163 = f32[3072,768]{1,0:T(8,128)} fusion(bf16[1024,3072]{1,0:T(8,128)(2,1)S(1)} %bitcast.272, bf16[1024,768]{0,1:T(8,128)(2,1)S(1)} %copy-done.73), kind=kOutput, calls=%fused_computation.437 | convolution fusion | flops 4831838208 | bytes 17301504 | tf_op jit(solution)/shard_map/ta,tb->ab/dot_general | solution.py:34
  333.1 5.2 add_convert_fusion.2
  343.1 3.0 copy.242
  346.2 3.4 concatenate.232
  352.0 3.1 fusion.161
  358.8 5.6 add_convert_fusion.1
  373.8 3.0 collective-permute-done.19
  378.3 2.7 collective-permute-done.20
  381.7 3.3 add_add_fusion.2
  385.0 3.7 copy.216
  406.3 4.2 collective-permute-done.43
  414.5 8.7 %collective-permute-done.23 = bf16[192,1536]{1,0:T(8,128)(2,1)S(1)} collective-permute-done((bf16[192,1536]{1,0:T(8,128)(2,1)S(1)}, bf16[192,1536]{1,0:T(8,128)(2,1)S(1)}, u32[]{:S(2)}, u32[]{:S(2)}) %collective-permute-start.23) | collective-permute-done | bytes 589856 | tf_op jit(solution)/shard_map/ppermute | solution.py:53
  427.1 8.7 %collective-permute-done.63 = bf16[384,768]{1,0:T(8,128)(2,1)S(1)} collective-permute-done((bf16[384,768]{1,0:T(8,128)(2,1)S(1)}, bf16[384,768]{1,0:T(8,128)(2,1)S(1)}, u32[]{:S(2)}, u32[]{:S(2)}) %collective-permute-start.63) | collective-permute-done | bytes 589856 | tf_op jit(solution)/shard_map/ppermute | solution.py:53
  439.8 4.6 collective-permute-done.44
  465.5 5.7 collective-permute-done.65
  479.2 5.2 collective-permute-done.11
  489.2 4.7 collective-permute-done.47
  505.1 3.1 collective-permute-done.38
  525.2 4.5 collective-permute-done.69
  529.7 2.7 collective-permute-start.30
  532.8 13.7 %collective-permute-done.50 = bf16[192,1536]{1,0:T(8,128)(2,1)S(1)} collective-permute-done((bf16[192,1536]{1,0:T(8,128)(2,1)S(1)}, bf16[192,1536]{1,0:T(8,128)(2,1)S(1)}, u32[]{:S(2)}, u32[]{:S(2)}) %collective-permute-start.50) | collective-permute-done | bytes 589856 | tf_op jit(solution)/shard_map/ppermute | solution.py:53
  548.6 22.2 %collective-permute-done.70 = bf16[384,768]{1,0:T(8,128)(2,1)S(1)} collective-permute-done((bf16[384,768]{1,0:T(8,128)(2,1)S(1)}, bf16[384,768]{1,0:T(8,128)(2,1)S(1)}, u32[]{:S(2)}, u32[]{:S(2)}) %collective-permute-start.70) | collective-permute-done | bytes 589856 | tf_op jit(solution)/shard_map/ppermute | solution.py:53
  574.6 10.8 %collective-permute-done.60 = bf16[384,768]{1,0:T(8,128)(2,1)S(1)} collective-permute-done((bf16[384,768]{1,0:T(8,128)(2,1)S(1)}, bf16[384,768]{1,0:T(8,128)(2,1)S(1)}, u32[]{:S(2)}, u32[]{:S(2)}) %collective-permute-start.60) | collective-permute-done | bytes 589856 | tf_op jit(solution)/shard_map/ppermute | solution.py:53
  595.1 4.5 maximum_convert_fusion.1
  600.3 5.0 maximum_convert_fusion
  (709 shorter events, 235.6 us)
Async XLA Ops:
  138.9 8.1 %collective-permute-start.3 = (bf16[2,4,768]{2,1,0:T(4,128)(2,1)S(1)}, bf16[2,4,768]{2,1,0:T(4,128)(2,1)S(1)}, u32[]{:S(2)}, u32[]{:S(2)}) collective-permute-start(bf16[2,4,768]{2,1,0:T(4,128)(2,1)S(1)} %pad_maximum_fusion), channel_id=1, source_target_pairs={{0,18},{1,19},{2,16},{3,17},{4,22},{5,23},{6,20},{7,21},{8,26},{9,... | collective-permute-start | bytes 36872 | tf_op jit(solution)/shard_map/ppermute | solution.py:53
  147.1 7.8 %collective-permute-start.4 = (bf16[8,4,768]{2,1,0:T(4,128)(2,1)S(1)}, bf16[8,4,768]{2,1,0:T(4,128)(2,1)S(1)}, u32[]{:S(2)}, u32[]{:S(2)}) collective-permute-start(bf16[8,4,768]{2,1,0:T(4,128)(2,1)S(1)} %get-tuple-element.484), channel_id=1, source_target_pairs={{0,4},{1,5},{2,6},{3,7},{4,0},{5,1},{6,2},{7,3},{8,12},{9,13},{10,... | collective-permute-start | bytes 147464 | tf_op jit(solution)/shard_map/ppermute | solution.py:53
  152.2 8.1 %collective-permute-start.6 = (bf16[8,4,768]{2,1,0:T(4,128)(2,1)S(1)}, bf16[8,4,768]{2,1,0:T(4,128)(2,1)S(1)}, u32[]{:S(2)}, u32[]{:S(2)}) collective-permute-start(bf16[8,4,768]{2,1,0:T(4,128)(2,1)S(1)} %get-tuple-element.484), channel_id=1, source_target_pairs={{0,12},{1,13},{2,14},{3,15},{4,8},{5,9},{6,10},{7,11},{8,4},{9,5},... | collective-permute-start | bytes 147464 | tf_op jit(solution)/shard_map/ppermute | solution.py:53
  342.0 49.6 %collective-permute-start.42 = (bf16[384,1536]{1,0:T(8,128)(2,1)}, bf16[384,1536]{1,0:T(8,128)(2,1)}, u32[]{:S(2)}, u32[]{:S(2)}) collective-permute-start(bf16[384,1536]{1,0:T(8,128)(2,1)} %constant_dynamic-slice_fusion.14), channel_id=1, source_target_pairs={{0,1},{1,0},{2,3},{3,2},{4,5},{5,4},{6,7},{7,6},{8,9},{9,8},{10,11... | collective-permute-start | bytes 3538952 | tf_op jit(solution)/shard_map/ppermute | solution.py:53
  342.0 52.3 %collective-permute-start.32 = (bf16[384,1536]{1,0:T(8,128)(2,1)}, bf16[384,1536]{1,0:T(8,128)(2,1)}, u32[]{:S(2)}, u32[]{:S(2)}) collective-permute-start(bf16[384,1536]{1,0:T(8,128)(2,1)} %constant_dynamic-slice_fusion.19), channel_id=1, source_target_pairs={{0,1},{1,0},{2,3},{3,2},{4,5},{5,4},{6,7},{7,6},{8,9},{9,8},{10,11... | collective-permute-start | bytes 3538952 | tf_op jit(solution)/shard_map/ppermute | solution.py:53
  349.6 17.8 %collective-permute-start.17 = (f32[12,768]{1,0:T(8,128)}, f32[12,768]{1,0:T(8,128)S(1)}, u32[]{:S(2)}, u32[]{:S(2)}) collective-permute-start(f32[12,768]{1,0:T(8,128)} %concatenate.232), channel_id=1, source_target_pairs={{0,1},{1,0},{2,3},{3,2},{4,5},{5,4},{6,7},{7,6},{8,9},{9,8},{10,11... | collective-permute-start | bytes 110600 | tf_op jit(solution)/shard_map/ppermute | solution.py:53
  367.0 29.4 %collective-permute-start.22 = (bf16[384,1536]{1,0:T(8,128)(2,1)}, bf16[384,1536]{1,0:T(8,128)(2,1)}, u32[]{:S(2)}, u32[]{:S(2)}) collective-permute-start(bf16[384,1536]{1,0:T(8,128)(2,1)} %fusion.75), channel_id=1, source_target_pairs={{0,1},{1,0},{2,3},{3,2},{4,5},{5,4},{6,7},{7,6},{8,9},{9,8},{10,11... | collective-permute-start | bytes 3538952 | tf_op jit(solution)/shard_map/ppermute | solution.py:53
  378.3 21.4 %collective-permute-start.7 = (bf16[384,1536]{1,0:T(8,128)(2,1)}, bf16[384,1536]{1,0:T(8,128)(2,1)}, u32[]{:S(2)}, u32[]{:S(2)}) collective-permute-start(bf16[384,1536]{1,0:T(8,128)(2,1)} %fusion.77), channel_id=1, source_target_pairs={{0,1},{1,0},{2,3},{3,2},{4,5},{5,4},{6,7},{7,6},{8,9},{9,8},{10,11... | collective-permute-start | bytes 3538952 | tf_op jit(solution)/shard_map/ppermute | solution.py:53
  381.6 7.7 %collective-permute-start.21 = (f32[12,768]{1,0:T(8,128)}, f32[12,768]{1,0:T(8,128)}, u32[]{:S(2)}, u32[]{:S(2)}) collective-permute-start(f32[12,768]{1,0:T(8,128)} %add.789), channel_id=1, source_target_pairs={{0,8},{1,9},{2,10},{3,11},{4,12},{5,13},{6,14},{7,15},{8,0},{9,1},... | collective-permute-start | bytes 110600 | tf_op jit(solution)/shard_map/ppermute | solution.py:53
  389.4 13.5 %collective-permute-start.62 = (bf16[768,768]{1,0:T(8,128)(2,1)}, bf16[768,768]{1,0:T(8,128)(2,1)}, u32[]{:S(2)}, u32[]{:S(2)}) collective-permute-start(bf16[768,768]{1,0:T(8,128)(2,1)} %constant_dynamic-slice_fusion.4), channel_id=1, source_target_pairs={{0,1},{1,0},{2,3},{3,2},{4,5},{5,4},{6,7},{7,6},{8,9},{9,8},{10,11... | collective-permute-start | bytes 3538952 | tf_op jit(solution)/shard_map/ppermute | solution.py:53
  391.6 13.7 %collective-permute-start.52 = (bf16[768,768]{1,0:T(8,128)(2,1)}, bf16[768,768]{1,0:T(8,128)(2,1)S(1)}, u32[]{:S(2)}, u32[]{:S(2)}) collective-permute-start(bf16[768,768]{1,0:T(8,128)(2,1)} %constant_dynamic-slice_fusion.9), channel_id=1, source_target_pairs={{0,1},{1,0},{2,3},{3,2},{4,5},{5,4},{6,7},{7,6},{8,9},{9,8},{10,11... | collective-permute-start | bytes 3538952 | tf_op jit(solution)/shard_map/ppermute | solution.py:53
  394.3 16.3 %collective-permute-start.43 = (bf16[192,1536]{1,0:T(8,128)(2,1)S(1)}, bf16[192,1536]{1,0:T(8,128)(2,1)S(1)}, u32[]{:S(2)}, u32[]{:S(2)}) collective-permute-start(bf16[192,1536]{1,0:T(8,128)(2,1)S(1)} %constant_dynamic-slice_fusion.13), channel_id=1, source_target_pairs={{0,2},{1,3},{2,0},{3,1},{4,6},{5,7},{6,4},{7,5},{8,10},{9,11},{10,... | collective-permute-start | bytes 1769480 | tf_op jit(solution)/shard_map/ppermute | solution.py:53
  396.5 16.3 %collective-permute-start.33 = (bf16[192,1536]{1,0:T(8,128)(2,1)S(1)}, bf16[192,1536]{1,0:T(8,128)(2,1)S(1)}, u32[]{:S(2)}, u32[]{:S(2)}) collective-permute-start(bf16[192,1536]{1,0:T(8,128)(2,1)S(1)} %constant_dynamic-slice_fusion.18), channel_id=1, source_target_pairs={{0,16},{1,17},{2,18},{3,19},{4,20},{5,21},{6,22},{7,23},{8,24},{9,... | collective-permute-start | bytes 1769480 | tf_op jit(solution)/shard_map/ppermute | solution.py:53
  399.7 23.5 %collective-permute-start.23 = (bf16[192,1536]{1,0:T(8,128)(2,1)S(1)}, bf16[192,1536]{1,0:T(8,128)(2,1)S(1)}, u32[]{:S(2)}, u32[]{:S(2)}) collective-permute-start(bf16[192,1536]{1,0:T(8,128)(2,1)S(1)} %constant_dynamic-slice_fusion.23), channel_id=1, source_target_pairs={{0,2},{1,3},{2,0},{3,1},{4,6},{5,7},{6,4},{7,5},{8,10},{9,11},{10,... | collective-permute-start | bytes 1769480 | tf_op jit(solution)/shard_map/ppermute | solution.py:53
  402.9 22.5 %collective-permute-start.8 = (bf16[192,1536]{1,0:T(8,128)(2,1)S(1)}, bf16[192,1536]{1,0:T(8,128)(2,1)S(1)}, u32[]{:S(2)}, u32[]{:S(2)}) collective-permute-start(bf16[192,1536]{1,0:T(8,128)(2,1)S(1)} %constant_dynamic-slice_fusion.27), channel_id=1, source_target_pairs={{0,16},{1,17},{2,18},{3,19},{4,20},{5,21},{6,22},{7,23},{8,24},{9,... | collective-permute-start | bytes 1769480 | tf_op jit(solution)/shard_map/ppermute | solution.py:53
  405.3 30.5 %collective-permute-start.63 = (bf16[384,768]{1,0:T(8,128)(2,1)S(1)}, bf16[384,768]{1,0:T(8,128)(2,1)S(1)}, u32[]{:S(2)}, u32[]{:S(2)}) collective-permute-start(bf16[384,768]{1,0:T(8,128)(2,1)S(1)} %constant_dynamic-slice_fusion.3), channel_id=1, source_target_pairs={{0,2},{1,3},{2,0},{3,1},{4,6},{5,7},{6,4},{7,5},{8,10},{9,11},{10,... | collective-permute-start | bytes 1769480 | tf_op jit(solution)/shard_map/ppermute | solution.py:53
  410.5 27.5 %collective-permute-start.53 = (bf16[384,768]{1,0:T(8,128)(2,1)S(1)}, bf16[384,768]{1,0:T(8,128)(2,1)S(1)}, u32[]{:S(2)}, u32[]{:S(2)}) collective-permute-start(bf16[384,768]{1,0:T(8,128)(2,1)S(1)} %constant_dynamic-slice_fusion.8), channel_id=1, source_target_pairs={{0,16},{1,17},{2,18},{3,19},{4,20},{5,21},{6,22},{7,23},{8,24},{9,... | collective-permute-start | bytes 1769480 | tf_op jit(solution)/shard_map/ppermute | solution.py:53
  412.8 31.6 %collective-permute-start.44 = (bf16[96,1536]{1,0:T(8,128)(2,1)S(1)}, bf16[96,1536]{1,0:T(8,128)(2,1)S(1)}, u32[]{:S(2)}, u32[]{:S(2)}) collective-permute-start(bf16[96,1536]{1,0:T(8,128)(2,1)S(1)} %constant_dynamic-slice_fusion.12), channel_id=1, source_target_pairs={{0,16},{1,17},{2,18},{3,19},{4,20},{5,21},{6,22},{7,23},{8,24},{9,... | collective-permute-start | bytes 884744 | tf_op jit(solution)/shard_map/ppermute | solution.py:53
  423.2 22.8 %collective-permute-start.34 = (bf16[96,1536]{1,0:T(8,128)(2,1)S(1)}, bf16[96,1536]{1,0:T(8,128)(2,1)S(1)}, u32[]{:S(2)}, u32[]{:S(2)}) collective-permute-start(bf16[96,1536]{1,0:T(8,128)(2,1)S(1)} %constant_dynamic-slice_fusion.17), channel_id=1, source_target_pairs={{0,2},{1,3},{2,0},{3,1},{4,6},{5,7},{6,4},{7,5},{8,10},{9,11},{10,... | collective-permute-start | bytes 884744 | tf_op jit(solution)/shard_map/ppermute | solution.py:53
  425.4 25.3 %collective-permute-start.24 = (bf16[96,1536]{1,0:T(8,128)(2,1)S(1)}, bf16[96,1536]{1,0:T(8,128)(2,1)S(1)}, u32[]{:S(2)}, u32[]{:S(2)}) collective-permute-start(bf16[96,1536]{1,0:T(8,128)(2,1)S(1)} %constant_dynamic-slice_fusion.22), channel_id=1, source_target_pairs={{0,16},{1,17},{2,18},{3,19},{4,20},{5,21},{6,22},{7,23},{8,24},{9,... | collective-permute-start | bytes 884744 | tf_op jit(solution)/shard_map/ppermute | solution.py:53
  435.8 16.9 %collective-permute-start.9 = (bf16[96,1536]{1,0:T(8,128)(2,1)S(1)}, bf16[96,1536]{1,0:T(8,128)(2,1)S(1)}, u32[]{:S(2)}, u32[]{:S(2)}) collective-permute-start(bf16[96,1536]{1,0:T(8,128)(2,1)S(1)} %constant_dynamic-slice_fusion.26), channel_id=1, source_target_pairs={{0,2},{1,3},{2,0},{3,1},{4,6},{5,7},{6,4},{7,5},{8,10},{9,11},{10,... | collective-permute-start | bytes 884744 | tf_op jit(solution)/shard_map/ppermute | solution.py:53
  438.1 17.7 %collective-permute-start.64 = (bf16[192,768]{1,0:T(8,128)(2,1)S(1)}, bf16[192,768]{1,0:T(8,128)(2,1)S(1)}, u32[]{:S(2)}, u32[]{:S(2)}) collective-permute-start(bf16[192,768]{1,0:T(8,128)(2,1)S(1)} %constant_dynamic-slice_fusion.2), channel_id=1, source_target_pairs={{0,16},{1,17},{2,18},{3,19},{4,20},{5,21},{6,22},{7,23},{8,24},{9,... | collective-permute-start | bytes 884744 | tf_op jit(solution)/shard_map/ppermute | solution.py:53
  444.4 13.4 %collective-permute-start.54 = (bf16[192,768]{1,0:T(8,128)(2,1)S(1)}, bf16[192,768]{1,0:T(8,128)(2,1)S(1)}, u32[]{:S(2)}, u32[]{:S(2)}) collective-permute-start(bf16[192,768]{1,0:T(8,128)(2,1)S(1)} %constant_dynamic-slice_fusion.7), channel_id=1, source_target_pairs={{0,2},{1,3},{2,0},{3,1},{4,6},{5,7},{6,4},{7,5},{8,10},{9,11},{10,... | collective-permute-start | bytes 884744 | tf_op jit(solution)/shard_map/ppermute | solution.py:53
  446.0 12.1 %collective-permute-start.45 = (bf16[48,1536]{1,0:T(8,128)(2,1)S(1)}, bf16[48,1536]{1,0:T(8,128)(2,1)S(1)}, u32[]{:S(2)}, u32[]{:S(2)}) collective-permute-start(bf16[48,1536]{1,0:T(8,128)(2,1)S(1)} %constant_dynamic-slice_fusion.11), channel_id=1, source_target_pairs={{0,4},{1,5},{2,6},{3,7},{4,0},{5,1},{6,2},{7,3},{8,12},{9,13},{10,... | collective-permute-start | bytes 442376 | tf_op jit(solution)/shard_map/ppermute | solution.py:53
  450.7 9.4 %collective-permute-start.35 = (bf16[48,1536]{1,0:T(8,128)(2,1)S(1)}, bf16[48,1536]{1,0:T(8,128)(2,1)S(1)}, u32[]{:S(2)}, u32[]{:S(2)}) collective-permute-start(bf16[48,1536]{1,0:T(8,128)(2,1)S(1)} %constant_dynamic-slice_fusion.16), channel_id=1, source_target_pairs={{0,4},{1,5},{2,6},{3,7},{4,0},{5,1},{6,2},{7,3},{8,12},{9,13},{10,... | collective-permute-start | bytes 442376 | tf_op jit(solution)/shard_map/ppermute | solution.py:53
  452.7 8.7 %collective-permute-start.25 = (bf16[48,1536]{1,0:T(8,128)(2,1)S(1)}, bf16[48,1536]{1,0:T(8,128)(2,1)S(1)}, u32[]{:S(2)}, u32[]{:S(2)}) collective-permute-start(bf16[48,1536]{1,0:T(8,128)(2,1)S(1)} %constant_dynamic-slice_fusion.21), channel_id=1, source_target_pairs={{0,4},{1,5},{2,6},{3,7},{4,0},{5,1},{6,2},{7,3},{8,12},{9,13},{10,... | collective-permute-start | bytes 442376 | tf_op jit(solution)/shard_map/ppermute | solution.py:53
  455.7 8.4 %collective-permute-start.10 = (bf16[48,1536]{1,0:T(8,128)(2,1)S(1)}, bf16[48,1536]{1,0:T(8,128)(2,1)S(1)}, u32[]{:S(2)}, u32[]{:S(2)}) collective-permute-start(bf16[48,1536]{1,0:T(8,128)(2,1)S(1)} %constant_dynamic-slice_fusion.25), channel_id=1, source_target_pairs={{0,4},{1,5},{2,6},{3,7},{4,0},{5,1},{6,2},{7,3},{8,12},{9,13},{10,... | collective-permute-start | bytes 442376 | tf_op jit(solution)/shard_map/ppermute | solution.py:53
  457.8 13.4 %collective-permute-start.65 = (bf16[96,768]{1,0:T(8,128)(2,1)S(1)}, bf16[96,768]{1,0:T(8,128)(2,1)S(1)}, u32[]{:S(2)}, u32[]{:S(2)}) collective-permute-start(bf16[96,768]{1,0:T(8,128)(2,1)S(1)} %constant_dynamic-slice_fusion.1), channel_id=1, source_target_pairs={{0,4},{1,5},{2,6},{3,7},{4,0},{5,1},{6,2},{7,3},{8,12},{9,13},{10,... | collective-permute-start | bytes 442376 | tf_op jit(solution)/shard_map/ppermute | solution.py:53
  458.1 14.9 %collective-permute-start.55 = (bf16[96,768]{1,0:T(8,128)(2,1)S(1)}, bf16[96,768]{1,0:T(8,128)(2,1)S(1)}, u32[]{:S(2)}, u32[]{:S(2)}) collective-permute-start(bf16[96,768]{1,0:T(8,128)(2,1)S(1)} %constant_dynamic-slice_fusion.6), channel_id=1, source_target_pairs={{0,4},{1,5},{2,6},{3,7},{4,0},{5,1},{6,2},{7,3},{8,12},{9,13},{10,... | collective-permute-start | bytes 442376 | tf_op jit(solution)/shard_map/ppermute | solution.py:53
  460.1 14.2 %collective-permute-start.46 = (bf16[24,1536]{1,0:T(8,128)(2,1)S(1)}, bf16[24,1536]{1,0:T(8,128)(2,1)S(1)}, u32[]{:S(2)}, u32[]{:S(2)}) collective-permute-start(bf16[24,1536]{1,0:T(8,128)(2,1)S(1)} %constant_dynamic-slice_fusion.10), channel_id=1, source_target_pairs={{0,8},{1,9},{2,10},{3,11},{4,12},{5,13},{6,14},{7,15},{8,0},{9,1},... | collective-permute-start | bytes 221192 | tf_op jit(solution)/shard_map/ppermute | solution.py:53
  461.5 14.6 %collective-permute-start.36 = (bf16[24,1536]{1,0:T(8,128)(2,1)S(1)}, bf16[24,1536]{1,0:T(8,128)(2,1)S(1)}, u32[]{:S(2)}, u32[]{:S(2)}) collective-permute-start(bf16[24,1536]{1,0:T(8,128)(2,1)S(1)} %constant_dynamic-slice_fusion.15), channel_id=1, source_target_pairs={{0,8},{1,9},{2,10},{3,11},{4,12},{5,13},{6,14},{7,15},{8,0},{9,1},... | collective-permute-start | bytes 221192 | tf_op jit(solution)/shard_map/ppermute | solution.py:53
  464.1 13.3 %collective-permute-start.26 = (bf16[24,1536]{1,0:T(8,128)(2,1)S(1)}, bf16[24,1536]{1,0:T(8,128)(2,1)S(1)}, u32[]{:S(2)}, u32[]{:S(2)}) collective-permute-start(bf16[24,1536]{1,0:T(8,128)(2,1)S(1)} %constant_dynamic-slice_fusion.20), channel_id=1, source_target_pairs={{0,8},{1,9},{2,10},{3,11},{4,12},{5,13},{6,14},{7,15},{8,0},{9,1},... | collective-permute-start | bytes 221192 | tf_op jit(solution)/shard_map/ppermute | solution.py:53
  471.2 13.2 %collective-permute-start.11 = (bf16[24,1536]{1,0:T(8,128)(2,1)S(1)}, bf16[24,1536]{1,0:T(8,128)(2,1)S(1)}, u32[]{:S(2)}, u32[]{:S(2)}) collective-permute-start(bf16[24,1536]{1,0:T(8,128)(2,1)S(1)} %constant_dynamic-slice_fusion.24), channel_id=1, source_target_pairs={{0,8},{1,9},{2,10},{3,11},{4,12},{5,13},{6,14},{7,15},{8,0},{9,1},... | collective-permute-start | bytes 221192 | tf_op jit(solution)/shard_map/ppermute | solution.py:53
  473.0 13.0 %collective-permute-start.66 = (bf16[48,768]{1,0:T(8,128)(2,1)S(1)}, bf16[48,768]{1,0:T(8,128)(2,1)S(1)}, u32[]{:S(2)}, u32[]{:S(2)}) collective-permute-start(bf16[48,768]{1,0:T(8,128)(2,1)S(1)} %constant_dynamic-slice_fusion), channel_id=1, source_target_pairs={{0,8},{1,9},{2,10},{3,11},{4,12},{5,13},{6,14},{7,15},{8,0},{9,1},... | collective-permute-start | bytes 221192 | tf_op jit(solution)/shard_map/ppermute | solution.py:53
  474.3 14.8 %collective-permute-start.56 = (bf16[48,768]{1,0:T(8,128)(2,1)S(1)}, bf16[48,768]{1,0:T(8,128)(2,1)S(1)}, u32[]{:S(2)}, u32[]{:S(2)}) collective-permute-start(bf16[48,768]{1,0:T(8,128)(2,1)S(1)} %constant_dynamic-slice_fusion.5), channel_id=1, source_target_pairs={{0,8},{1,9},{2,10},{3,11},{4,12},{5,13},{6,14},{7,15},{8,0},{9,1},... | collective-permute-start | bytes 221192 | tf_op jit(solution)/shard_map/ppermute | solution.py:53
  476.1 17.8 %collective-permute-start.47 = (bf16[24,1536]{1,0:T(8,128)(2,1)S(1)}, bf16[24,1536]{1,0:T(8,128)(2,1)S(1)}, u32[]{:S(2)}, u32[]{:S(2)}) collective-permute-start(bf16[24,1536]{1,0:T(8,128)(2,1)S(1)} %add_convert_fusion.40), channel_id=1, source_target_pairs={{0,8},{1,9},{2,10},{3,11},{4,12},{5,13},{6,14},{7,15},{8,0},{9,1},... | collective-permute-start | bytes 221192 | tf_op jit(solution)/shard_map/ppermute | solution.py:53
  477.5 18.0 %collective-permute-start.37 = (bf16[24,1536]{1,0:T(8,128)(2,1)S(1)}, bf16[24,1536]{1,0:T(8,128)(2,1)S(1)}, u32[]{:S(2)}, u32[]{:S(2)}) collective-permute-start(bf16[24,1536]{1,0:T(8,128)(2,1)S(1)} %add_convert_fusion.41), channel_id=1, source_target_pairs={{0,8},{1,9},{2,10},{3,11},{4,12},{5,13},{6,14},{7,15},{8,0},{9,1},... | collective-permute-start | bytes 221192 | tf_op jit(solution)/shard_map/ppermute | solution.py:53
  484.4 12.7 %collective-permute-start.27 = (bf16[24,1536]{1,0:T(8,128)(2,1)S(1)}, bf16[24,1536]{1,0:T(8,128)(2,1)S(1)}, u32[]{:S(2)}, u32[]{:S(2)}) collective-permute-start(bf16[24,1536]{1,0:T(8,128)(2,1)S(1)} %add_convert_fusion.42), channel_id=1, source_target_pairs={{0,8},{1,9},{2,10},{3,11},{4,12},{5,13},{6,14},{7,15},{8,0},{9,1},... | collective-permute-start | bytes 221192 | tf_op jit(solution)/shard_map/ppermute | solution.py:53
  486.0 13.5 %collective-permute-start.12 = (bf16[24,1536]{1,0:T(8,128)(2,1)S(1)}, bf16[24,1536]{1,0:T(8,128)(2,1)S(1)}, u32[]{:S(2)}, u32[]{:S(2)}) collective-permute-start(bf16[24,1536]{1,0:T(8,128)(2,1)S(1)} %add_convert_fusion.43), channel_id=1, source_target_pairs={{0,8},{1,9},{2,10},{3,11},{4,12},{5,13},{6,14},{7,15},{8,0},{9,1},... | collective-permute-start | bytes 221192 | tf_op jit(solution)/shard_map/ppermute | solution.py:53
  489.2 11.9 %collective-permute-start.67 = (bf16[48,768]{1,0:T(8,128)(2,1)S(1)}, bf16[48,768]{1,0:T(8,128)(2,1)S(1)}, u32[]{:S(2)}, u32[]{:S(2)}) collective-permute-start(bf16[48,768]{1,0:T(8,128)(2,1)S(1)} %add_convert_fusion.38), channel_id=1, source_target_pairs={{0,8},{1,9},{2,10},{3,11},{4,12},{5,13},{6,14},{7,15},{8,0},{9,1},... | collective-permute-start | bytes 221192 | tf_op jit(solution)/shard_map/ppermute | solution.py:53
  493.9 7.9 %collective-permute-start.57 = (bf16[48,768]{1,0:T(8,128)(2,1)S(1)}, bf16[48,768]{1,0:T(8,128)(2,1)S(1)}, u32[]{:S(2)}, u32[]{:S(2)}) collective-permute-start(bf16[48,768]{1,0:T(8,128)(2,1)S(1)} %add_convert_fusion.39), channel_id=1, source_target_pairs={{0,8},{1,9},{2,10},{3,11},{4,12},{5,13},{6,14},{7,15},{8,0},{9,1},... | collective-permute-start | bytes 221192 | tf_op jit(solution)/shard_map/ppermute | solution.py:53
  495.5 9.5 %collective-permute-start.48 = (bf16[48,1536]{1,0:T(8,128)(2,1)S(1)}, bf16[48,1536]{1,0:T(8,128)(2,1)S(1)}, u32[]{:S(2)}, u32[]{:S(2)}) collective-permute-start(bf16[48,1536]{1,0:T(8,128)(2,1)S(1)} %maximum_select_fusion.27), channel_id=1, source_target_pairs={{0,4},{1,5},{2,6},{3,7},{4,0},{5,1},{6,2},{7,3},{8,12},{9,13},{10,... | collective-permute-start | bytes 442376 | tf_op jit(solution)/shard_map/ppermute | solution.py:53
  497.1 11.1 %collective-permute-start.38 = (bf16[48,1536]{1,0:T(8,128)(2,1)S(1)}, bf16[48,1536]{1,0:T(8,128)(2,1)S(1)}, u32[]{:S(2)}, u32[]{:S(2)}) collective-permute-start(bf16[48,1536]{1,0:T(8,128)(2,1)S(1)} %maximum_select_fusion.26), channel_id=1, source_target_pairs={{0,4},{1,5},{2,6},{3,7},{4,0},{5,1},{6,2},{7,3},{8,12},{9,13},{10,... | collective-permute-start | bytes 442376 | tf_op jit(solution)/shard_map/ppermute | solution.py:53
  499.5 11.8 %collective-permute-start.28 = (bf16[48,1536]{1,0:T(8,128)(2,1)S(1)}, bf16[48,1536]{1,0:T(8,128)(2,1)S(1)}, u32[]{:S(2)}, u32[]{:S(2)}) collective-permute-start(bf16[48,1536]{1,0:T(8,128)(2,1)S(1)} %maximum_select_fusion.25), channel_id=1, source_target_pairs={{0,4},{1,5},{2,6},{3,7},{4,0},{5,1},{6,2},{7,3},{8,12},{9,13},{10,... | collective-permute-start | bytes 442376 | tf_op jit(solution)/shard_map/ppermute | solution.py:53
  501.0 13.5 %collective-permute-start.13 = (bf16[48,1536]{1,0:T(8,128)(2,1)S(1)}, bf16[48,1536]{1,0:T(8,128)(2,1)S(1)}, u32[]{:S(2)}, u32[]{:S(2)}) collective-permute-start(bf16[48,1536]{1,0:T(8,128)(2,1)S(1)} %maximum_select_fusion.24), channel_id=1, source_target_pairs={{0,4},{1,5},{2,6},{3,7},{4,0},{5,1},{6,2},{7,3},{8,12},{9,13},{10,... | collective-permute-start | bytes 442376 | tf_op jit(solution)/shard_map/ppermute | solution.py:53
  501.8 15.8 %collective-permute-start.68 = (bf16[96,768]{1,0:T(8,128)(2,1)S(1)}, bf16[96,768]{1,0:T(8,128)(2,1)S(1)}, u32[]{:S(2)}, u32[]{:S(2)}) collective-permute-start(bf16[96,768]{1,0:T(8,128)(2,1)S(1)} %maximum_select_fusion.29), channel_id=1, source_target_pairs={{0,4},{1,5},{2,6},{3,7},{4,0},{5,1},{6,2},{7,3},{8,12},{9,13},{10,... | collective-permute-start | bytes 442376 | tf_op jit(solution)/shard_map/ppermute | solution.py:53
  505.0 14.9 %collective-permute-start.58 = (bf16[96,768]{1,0:T(8,128)(2,1)S(1)}, bf16[96,768]{1,0:T(8,128)(2,1)S(1)}, u32[]{:S(2)}, u32[]{:S(2)}) collective-permute-start(bf16[96,768]{1,0:T(8,128)(2,1)S(1)} %maximum_select_fusion.28), channel_id=1, source_target_pairs={{0,4},{1,5},{2,6},{3,7},{4,0},{5,1},{6,2},{7,3},{8,12},{9,13},{10,... | collective-permute-start | bytes 442376 | tf_op jit(solution)/shard_map/ppermute | solution.py:53
  508.2 13.3 %collective-permute-start.49 = (bf16[96,1536]{1,0:T(8,128)(2,1)S(1)}, bf16[96,1536]{1,0:T(8,128)(2,1)S(1)}, u32[]{:S(2)}, u32[]{:S(2)}) collective-permute-start(bf16[96,1536]{1,0:T(8,128)(2,1)S(1)} %maximum_select_fusion.21), channel_id=1, source_target_pairs={{0,16},{1,17},{2,18},{3,19},{4,20},{5,21},{6,22},{7,23},{8,24},{9,... | collective-permute-start | bytes 884744 | tf_op jit(solution)/shard_map/ppermute | solution.py:53
  511.3 12.9 %collective-permute-start.39 = (bf16[96,1536]{1,0:T(8,128)(2,1)S(1)}, bf16[96,1536]{1,0:T(8,128)(2,1)S(1)}, u32[]{:S(2)}, u32[]{:S(2)}) collective-permute-start(bf16[96,1536]{1,0:T(8,128)(2,1)S(1)} %maximum_select_fusion.20), channel_id=1, source_target_pairs={{0,2},{1,3},{2,0},{3,1},{4,6},{5,7},{6,4},{7,5},{8,10},{9,11},{10,... | collective-permute-start | bytes 884744 | tf_op jit(solution)/shard_map/ppermute | solution.py:53
  514.5 10.0 %collective-permute-start.29 = (bf16[96,1536]{1,0:T(8,128)(2,1)S(1)}, bf16[96,1536]{1,0:T(8,128)(2,1)S(1)}, u32[]{:S(2)}, u32[]{:S(2)}) collective-permute-start(bf16[96,1536]{1,0:T(8,128)(2,1)S(1)} %maximum_select_fusion.19), channel_id=1, source_target_pairs={{0,16},{1,17},{2,18},{3,19},{4,20},{5,21},{6,22},{7,23},{8,24},{9,... | collective-permute-start | bytes 884744 | tf_op jit(solution)/shard_map/ppermute | solution.py:53
  517.6 15.0 %collective-permute-start.14 = (bf16[96,1536]{1,0:T(8,128)(2,1)S(1)}, bf16[96,1536]{1,0:T(8,128)(2,1)S(1)}, u32[]{:S(2)}, u32[]{:S(2)}) collective-permute-start(bf16[96,1536]{1,0:T(8,128)(2,1)S(1)} %maximum_select_fusion.18), channel_id=1, source_target_pairs={{0,2},{1,3},{2,0},{3,1},{4,6},{5,7},{6,4},{7,5},{8,10},{9,11},{10,... | collective-permute-start | bytes 884744 | tf_op jit(solution)/shard_map/ppermute | solution.py:53
  519.9 9.8 %collective-permute-start.69 = (bf16[192,768]{1,0:T(8,128)(2,1)S(1)}, bf16[192,768]{1,0:T(8,128)(2,1)S(1)}, u32[]{:S(2)}, u32[]{:S(2)}) collective-permute-start(bf16[192,768]{1,0:T(8,128)(2,1)S(1)} %maximum_select_fusion.23), channel_id=1, source_target_pairs={{0,16},{1,17},{2,18},{3,19},{4,20},{5,21},{6,22},{7,23},{8,24},{9,... | collective-permute-start | bytes 884744 | tf_op jit(solution)/shard_map/ppermute | solution.py:53
  521.5 26.9 %collective-permute-start.59 = (bf16[192,768]{1,0:T(8,128)(2,1)S(1)}, bf16[192,768]{1,0:T(8,128)(2,1)S(1)}, u32[]{:S(2)}, u32[]{:S(2)}) collective-permute-start(bf16[192,768]{1,0:T(8,128)(2,1)S(1)} %maximum_select_fusion.22), channel_id=1, source_target_pairs={{0,2},{1,3},{2,0},{3,1},{4,6},{5,7},{6,4},{7,5},{8,10},{9,11},{10,... | collective-permute-start | bytes 884744 | tf_op jit(solution)/shard_map/ppermute | solution.py:53
  524.3 22.2 %collective-permute-start.50 = (bf16[192,1536]{1,0:T(8,128)(2,1)S(1)}, bf16[192,1536]{1,0:T(8,128)(2,1)S(1)}, u32[]{:S(2)}, u32[]{:S(2)}) collective-permute-start(bf16[192,1536]{1,0:T(8,128)(2,1)S(1)} %maximum_select_fusion.15), channel_id=1, source_target_pairs={{0,2},{1,3},{2,0},{3,1},{4,6},{5,7},{6,4},{7,5},{8,10},{9,11},{10,... | collective-permute-start | bytes 1769480 | tf_op jit(solution)/shard_map/ppermute | solution.py:53
  524.5 49.7 %collective-permute-start.40 = (bf16[192,1536]{1,0:T(8,128)(2,1)S(1)}, bf16[192,1536]{1,0:T(8,128)(2,1)S(1)}, u32[]{:S(2)}, u32[]{:S(2)}) collective-permute-start(bf16[192,1536]{1,0:T(8,128)(2,1)S(1)} %maximum_select_fusion.14), channel_id=1, source_target_pairs={{0,16},{1,17},{2,18},{3,19},{4,20},{5,21},{6,22},{7,23},{8,24},{9,... | collective-permute-start | bytes 1769480 | tf_op jit(solution)/shard_map/ppermute | solution.py:53
  529.7 43.0 %collective-permute-start.30 = (bf16[192,1536]{1,0:T(8,128)(2,1)S(1)}, bf16[192,1536]{1,0:T(8,128)(2,1)S(1)}, u32[]{:S(2)}, u32[]{:S(2)}) collective-permute-start(bf16[192,1536]{1,0:T(8,128)(2,1)S(1)} %maximum_select_fusion.13), channel_id=1, source_target_pairs={{0,2},{1,3},{2,0},{3,1},{4,6},{5,7},{6,4},{7,5},{8,10},{9,11},{10,... | collective-permute-start | bytes 1769480 | tf_op jit(solution)/shard_map/ppermute | solution.py:53
  532.6 38.2 %collective-permute-start.70 = (bf16[384,768]{1,0:T(8,128)(2,1)S(1)}, bf16[384,768]{1,0:T(8,128)(2,1)S(1)}, u32[]{:S(2)}, u32[]{:S(2)}) collective-permute-start(bf16[384,768]{1,0:T(8,128)(2,1)S(1)} %maximum_select_fusion.17), channel_id=1, source_target_pairs={{0,2},{1,3},{2,0},{3,1},{4,6},{5,7},{6,4},{7,5},{8,10},{9,11},{10,... | collective-permute-start | bytes 1769480 | tf_op jit(solution)/shard_map/ppermute | solution.py:53
  546.5 26.7 %collective-permute-start.15 = (bf16[192,1536]{1,0:T(8,128)(2,1)S(1)}, bf16[192,1536]{1,0:T(8,128)(2,1)S(1)}, u32[]{:S(2)}, u32[]{:S(2)}) collective-permute-start(bf16[192,1536]{1,0:T(8,128)(2,1)S(1)} %maximum_select_fusion.12), channel_id=1, source_target_pairs={{0,16},{1,17},{2,18},{3,19},{4,20},{5,21},{6,22},{7,23},{8,24},{9,... | collective-permute-start | bytes 1769480 | tf_op jit(solution)/shard_map/ppermute | solution.py:53
  548.4 37.6 %collective-permute-start.51 = (bf16[384,1536]{1,0:T(8,128)(2,1)S(1)}, bf16[384,1536]{1,0:T(8,128)(2,1)S(1)}, u32[]{:S(2)}, u32[]{:S(2)}) collective-permute-start(bf16[384,1536]{1,0:T(8,128)(2,1)S(1)} %maximum_select_fusion.9), channel_id=1, source_target_pairs={{0,1},{1,0},{2,3},{3,2},{4,5},{5,4},{6,7},{7,6},{8,9},{9,8},{10,11... | collective-permute-start | bytes 3538952 | tf_op jit(solution)/shard_map/ppermute | solution.py:53
  570.8 14.6 %collective-permute-start.60 = (bf16[384,768]{1,0:T(8,128)(2,1)S(1)}, bf16[384,768]{1,0:T(8,128)(2,1)S(1)}, u32[]{:S(2)}, u32[]{:S(2)}) collective-permute-start(bf16[384,768]{1,0:T(8,128)(2,1)S(1)} %maximum_select_fusion.16), channel_id=1, source_target_pairs={{0,16},{1,17},{2,18},{3,19},{4,20},{5,21},{6,22},{7,23},{8,24},{9,... | collective-permute-start | bytes 1769480 | tf_op jit(solution)/shard_map/ppermute | solution.py:53
  572.7 14.5 %collective-permute-start.71 = (bf16[768,768]{1,0:T(8,128)(2,1)S(1)}, bf16[768,768]{1,0:T(8,128)(2,1)S(1)}, u32[]{:S(2)}, u32[]{:S(2)}) collective-permute-start(bf16[768,768]{1,0:T(8,128)(2,1)S(1)} %maximum_select_fusion.11), channel_id=1, source_target_pairs={{0,1},{1,0},{2,3},{3,2},{4,5},{5,4},{6,7},{7,6},{8,9},{9,8},{10,11... | collective-permute-start | bytes 3538952 | tf_op jit(solution)/shard_map/ppermute | solution.py:53
  573.2 14.8 %collective-permute-start.31 = (bf16[384,1536]{1,0:T(8,128)(2,1)S(1)}, bf16[384,1536]{1,0:T(8,128)(2,1)S(1)}, u32[]{:S(2)}, u32[]{:S(2)}) collective-permute-start(bf16[384,1536]{1,0:T(8,128)(2,1)S(1)} %maximum_select_fusion.7), channel_id=1, source_target_pairs={{0,1},{1,0},{2,3},{3,2},{4,5},{5,4},{6,7},{7,6},{8,9},{9,8},{10,11... | collective-permute-start | bytes 3538952 | tf_op jit(solution)/shard_map/ppermute | solution.py:53
  574.1 14.5 %collective-permute-start.16 = (bf16[384,1536]{1,0:T(8,128)(2,1)S(1)}, bf16[384,1536]{1,0:T(8,128)(2,1)S(1)}, u32[]{:S(2)}, u32[]{:S(2)}) collective-permute-start(bf16[384,1536]{1,0:T(8,128)(2,1)S(1)} %maximum_select_fusion.6), channel_id=1, source_target_pairs={{0,1},{1,0},{2,3},{3,2},{4,5},{5,4},{6,7},{7,6},{8,9},{9,8},{10,11... | collective-permute-start | bytes 3538952 | tf_op jit(solution)/shard_map/ppermute | solution.py:53
  585.4 14.2 %collective-permute-start.41 = (bf16[384,1536]{1,0:T(8,128)(2,1)S(1)}, bf16[384,1536]{1,0:T(8,128)(2,1)S(1)}, u32[]{:S(2)}, u32[]{:S(2)}) collective-permute-start(bf16[384,1536]{1,0:T(8,128)(2,1)S(1)} %maximum_select_fusion.8), channel_id=1, source_target_pairs={{0,1},{1,0},{2,3},{3,2},{4,5},{5,4},{6,7},{7,6},{8,9},{9,8},{10,11... | collective-permute-start | bytes 3538952 | tf_op jit(solution)/shard_map/ppermute | solution.py:53
  (165 other events, 1174.0 us)
